TPU v7x, 32 devices: a whole 2x2x4 slice. The times are simulated.
32 devices in a mesh: wide: 8 (over z, core), narrow: 4 (over y, x).
Axes of the slice: x: 2, y: 2, z: 4, core: 2. Of those that a mesh axis runs over, the one named last changes fastest.
Arguments:
- tokens: bfloat16 [8192, 768], P(('wide', 'narrow')), may hold values from -6 to 6
- timestep: float32 [4, 768], replicated, may hold values from -6 to 6
- clip_lengths: int32 [4], replicated, may hold values from 1 to 16, 32 in all
- pad_mask: int32 [32, 256], replicated, may hold values 0 or 1
- spacemodulation: bfloat16 [768, 4608], P(('wide', 'narrow')), may hold values from -0.21875 to 0.21875
- spaceoffsets: bfloat16 [4608], P(('wide', 'narrow')), may hold values from -3 to 3
- spacemixing: bfloat16 [768, 2304], P(('wide', 'narrow')), may hold values from -0.21875 to 0.21875
- spaceoutput: bfloat16 [768, 768], P(('wide', 'narrow')), may hold values from -0.875 to 0.875
- spaceexpand: bfloat16 [768, 3072], P(('wide', 'narrow')), may hold values from -0.21875 to 0.21875
- spacereduce: bfloat16 [3072, 768], P(('wide', 'narrow')), may hold values from -0.109375 to 0.109375
- timemodulation: bfloat16 [768, 4608], P(('wide', 'narrow')), may hold values from -0.21875 to 0.21875
- timeoffsets: bfloat16 [4608], P(('wide', 'narrow')), may hold values from -3 to 3
- timemixing: bfloat16 [768, 2304], P(('wide', 'narrow')), may hold values from -0.21875 to 0.21875
- timeoutput: bfloat16 [768, 768], P(('wide', 'narrow')), may hold values from -0.4375 to 0.4375
- timeexpand: bfloat16 [768, 3072], P(('wide', 'narrow')), may hold values from -0.21875 to 0.21875
- timereduce: bfloat16 [3072, 768], P(('wide', 'narrow')), may hold values from -0.109375 to 0.109375
- cotangent: bfloat16 [8192, 768], P(('wide', 'narrow')), may hold values from -6 to 6
Outputs:
- first_block: float32 [8192, 768], P(('wide', 'narrow'))
- second_block: float32 [8192, 768], P(('wide', 'narrow'))
- input_grad: float32 [8192, 768], P(('wide', 'narrow'))
- spacemodulation_grad: float32 [768, 4608], P(('wide', 'narrow'))
- spaceoffsets_grad: float32 [4608], P(('wide', 'narrow'))
- spacemixing_grad: float32 [768, 2304], P(('wide', 'narrow'))
- spaceoutput_grad: float32 [768, 768], P(('wide', 'narrow'))
- spaceexpand_grad: float32 [768, 3072], P(('wide', 'narrow'))
- spacereduce_grad: float32 [3072, 768], P(('wide', 'narrow'))
- timemodulation_grad: float32 [768, 4608], P(('wide', 'narrow'))
- timeoffsets_grad: float32 [4608], P(('wide', 'narrow'))
- timemixing_grad: float32 [768, 2304], P(('wide', 'narrow'))
- timeoutput_grad: float32 [768, 768], P(('wide', 'narrow'))
- timeexpand_grad: float32 [768, 3072], P(('wide', 'narrow'))
- timereduce_grad: float32 [3072, 768], P(('wide', 'narrow'))
Inputs may be any that keep to these rules, and one draw needn't show every extreme that they name: `clip_lengths`: the clip lengths sum to 32; clips lie one after the other in frame order.
All inputs are finite; a program needn't handle non-finite values.
Results may differ from a plain program's by a relative error of at most 0.018.
The roundings to bfloat16 on the way count: a program that leaves them out, or rounds other values in their place, can miss the bound.
Values may be sent and summed in bfloat16 or wider, within the bound.
A program may use at most 192 MiB of HBM per device.

v0:
```python
import jax
import jax.numpy as jnp
from jax import lax
from jax.sharding import PartitionSpec as P

HEADS = 12


def layer_norm(value):
    centred = value - jnp.mean(value, axis=-1, keepdims=True)
    spread = jnp.mean(centred * centred, axis=-1, keepdims=True)
    return centred * lax.rsqrt(spread + 1e-06)


def modulate(value, scale, shift):
    return layer_norm(value) * (1.0 + scale) + shift


def gelu_tanh(value):
    return jax.nn.gelu(value, approximate=True)


def against(left, weight):
    return lax.dot_general(
        left, weight, (((left.ndim - 1,), (1,)), ((), ())), preferred_element_type=jnp.float32
    )


def outer(left, right):
    return jnp.einsum("fpa,fpb->ab", left, right, preferred_element_type=jnp.float32)


def layouts(layout):
    return (layout.replace("x", "q") + "hd", layout.replace("x", "k") + "hd")


def split_heads(mixing):
    parts = mixing.reshape(
        mixing.shape[0], mixing.shape[1], 3, HEADS, mixing.shape[2] // (3 * HEADS)
    )
    return (parts[:, :, 0], parts[:, :, 1], parts[:, :, 2])


def masked_scores(queries, keys, allowed, layout):
    query_form, key_form = layouts(layout)
    scale = queries.shape[-1] ** (-0.5)
    scores = (
        jnp.einsum(
            query_form + "," + key_form + "->ghqk",
            queries,
            keys,
            preferred_element_type=jnp.float32,
        )
        * scale
    )
    return jnp.where(allowed[:, None], scores, -1e30)


def attention_forward(mixing, allowed, layout):
    queries, keys, values = split_heads(mixing)
    query_form, key_form = layouts(layout)
    scores = masked_scores(queries, keys, allowed, layout)
    top = jnp.max(scores, axis=-1, keepdims=True)
    expo = jnp.exp(scores - top)
    total = jnp.sum(expo, axis=-1, keepdims=True)
    probs = (expo / total).astype(jnp.bfloat16)
    logsum = top + jnp.log(total)
    result = jnp.einsum(
        "ghqk," + key_form + "->" + query_form, probs, values, preferred_element_type=jnp.float32
    )
    result = result.astype(jnp.bfloat16).reshape(mixing.shape[0], mixing.shape[1], -1)
    return (result, (mixing, logsum))


def attention_backward(state, grad_attended, allowed, layout):
    mixing, logsum = state
    queries, keys, values = split_heads(mixing)
    query_form, key_form = layouts(layout)
    grad_result = grad_attended.reshape(queries.shape)
    exact = jnp.exp(masked_scores(queries, keys, allowed, layout) - logsum)
    probs = exact.astype(jnp.bfloat16)
    grad_values = jnp.einsum(
        "ghqk," + query_form + "->" + key_form,
        probs,
        grad_result,
        preferred_element_type=jnp.float32,
    )
    grad_probs = jnp.einsum(
        query_form + "," + key_form + "->ghqk",
        grad_result,
        values,
        preferred_element_type=jnp.float32,
    )
    grad_scores = exact * (grad_probs - jnp.sum(grad_probs * exact, axis=-1, keepdims=True))
    grad_scores = grad_scores.astype(jnp.bfloat16)
    scale = queries.shape[-1] ** (-0.5)
    grad_queries = (
        jnp.einsum(
            "ghqk," + key_form + "->" + query_form,
            grad_scores,
            keys,
            preferred_element_type=jnp.float32,
        )
        * scale
    )
    grad_keys = (
        jnp.einsum(
            "ghqk," + query_form + "->" + key_form,
            grad_scores,
            queries,
            preferred_element_type=jnp.float32,
        )
        * scale
    )
    stacked = jnp.stack([grad_queries, grad_keys, grad_values], axis=2)
    return stacked.reshape(mixing.shape).astype(jnp.bfloat16)


def forward(inputs, weights, cond, onehot_own, mixer):
    w_mod, w_bias, w_mix, w_out, w_up, w_down = weights
    table = jnp.dot(cond, w_mod, preferred_element_type=jnp.float32) + w_bias.astype(jnp.float32)
    mods = jnp.dot(onehot_own, table, precision=lax.Precision.HIGHEST)[:, None, :]
    pieces = jnp.split(mods, 6, axis=2)
    normed = modulate(inputs, pieces[1], pieces[0]).astype(jnp.bfloat16)
    mixing = jnp.dot(normed, w_mix, preferred_element_type=jnp.float32).astype(jnp.bfloat16)
    attended, state = mixer[0](mixing)
    branch = jnp.dot(attended, w_out, preferred_element_type=jnp.float32)
    middle = inputs + pieces[2] * branch
    normed_b = modulate(middle, pieces[4], pieces[3]).astype(jnp.bfloat16)
    hidden = jnp.dot(normed_b, w_up, preferred_element_type=jnp.float32)
    active = gelu_tanh(hidden).astype(jnp.bfloat16)
    out = jnp.dot(active, w_down, preferred_element_type=jnp.float32)
    result = middle + pieces[5] * out
    return (
        result,
        (inputs, pieces, normed, state, attended, branch, middle, normed_b, hidden, active, out),
    )


def backward(kept, weights, grad, cond, onehot_own, mixer, here, devices):
    inputs, pieces, normed, state, attended, branch, middle, normed_b, hidden, active, out = kept
    w_mod, w_bias, w_mix, w_out, w_up, w_down = weights
    grad_out = (pieces[5] * grad).astype(jnp.bfloat16)
    grad_gate_b = jnp.sum(out * grad, axis=1, keepdims=True)
    grad_down = outer(active, grad_out)
    grad_active = against(grad_out, w_down)
    grad_hidden = jax.vjp(gelu_tanh, hidden)[1](grad_active)[0].astype(jnp.bfloat16)
    grad_up = outer(normed_b, grad_hidden)
    grad_normed_b = against(grad_hidden, w_up)
    part_middle, grad_scale_b, grad_shift_b = jax.vjp(modulate, middle, pieces[4], pieces[3])[1](
        grad_normed_b
    )
    grad_middle = grad + part_middle
    grad_branch = (pieces[2] * grad_middle).astype(jnp.bfloat16)
    grad_gate_a = jnp.sum(branch * grad_middle, axis=1, keepdims=True)
    grad_output = outer(attended, grad_branch)
    grad_attended = against(grad_branch, w_out).astype(jnp.bfloat16)
    grad_mixing = mixer[1](state, grad_attended)
    grad_project = outer(normed, grad_mixing)
    grad_normed = against(grad_mixing, w_mix)
    part_input, grad_scale_a, grad_shift_a = jax.vjp(modulate, inputs, pieces[1], pieces[0])[1](
        grad_normed
    )
    grad_input = grad_middle + part_input
    grad_frames = jnp.concatenate(
        [grad_shift_a, grad_scale_a, grad_gate_a, grad_shift_b, grad_scale_b, grad_gate_b], axis=2
    )[:, 0]
    grad_table = lax.dot_general(
        onehot_own, grad_frames, (((0,), (0,)), ((), ())), precision=lax.Precision.HIGHEST
    )
    summed = lax.psum(grad_table, ("wide", "narrow")).astype(jnp.bfloat16)
    row_count = w_mod.shape[0] // devices
    cond_rows = lax.dynamic_slice_in_dim(cond, here * row_count, row_count, 1)
    grad_mod = lax.dot_general(
        cond_rows, summed, (((0,), (0,)), ((), ())), preferred_element_type=jnp.float32
    )
    bias_count = w_bias.shape[0] // devices
    grad_bias = lax.dynamic_slice_in_dim(
        jnp.sum(summed.astype(jnp.float32), axis=0), here * bias_count, bias_count, 0
    )
    owned = (
        lax.psum_scatter(grad_project, ("wide", "narrow"), scatter_dimension=0, tiled=True),
        lax.psum_scatter(grad_output, ("wide", "narrow"), scatter_dimension=0, tiled=True),
        lax.psum_scatter(grad_up, ("wide", "narrow"), scatter_dimension=0, tiled=True),
        lax.psum_scatter(grad_down, ("wide", "narrow"), scatter_dimension=0, tiled=True),
    )
    return (grad_input, (grad_mod, grad_bias, owned[0], owned[1], owned[2], owned[3]))


def fetch(shards):
    return (
        lax.all_gather(shards[0], ("wide", "narrow"), axis=0, tiled=True),
        lax.all_gather(shards[1], ("wide", "narrow"), axis=0, tiled=True),
        lax.all_gather(shards[2], ("wide", "narrow"), axis=0, tiled=True),
        lax.all_gather(shards[3], ("wide", "narrow"), axis=0, tiled=True),
        lax.all_gather(shards[4], ("wide", "narrow"), axis=0, tiled=True),
        lax.all_gather(shards[5], ("wide", "narrow"), axis=0, tiled=True),
    )


def per_device(
    tokens,
    timestep,
    clip_lengths,
    pad_mask,
    spacemodulation,
    spaceoffsets,
    spacemixing,
    spaceoutput,
    spaceexpand,
    spacereduce,
    timemodulation,
    timeoffsets,
    timemixing,
    timeoutput,
    timeexpand,
    timereduce,
    cotangent,
):
    devices = lax.axis_size(("wide", "narrow"))
    here = lax.axis_index(("wide", "narrow"))
    patches = pad_mask.shape[1]
    frames_own = tokens.shape[0] // patches
    frames_all = pad_mask.shape[0]
    width = tokens.shape[1]
    ends = jnp.cumsum(clip_lengths)
    segment = jnp.sum(
        (ends[None, :] <= jnp.arange(frames_all, dtype=jnp.int32)[:, None]).astype(jnp.int32),
        axis=1,
    )
    onehot_all = (
        segment[:, None] == jnp.arange(clip_lengths.shape[0], dtype=jnp.int32)[None, :]
    ).astype(jnp.float32)
    onehot_own = lax.dynamic_slice_in_dim(onehot_all, here * frames_own, frames_own, 0)
    keep_own = lax.dynamic_slice_in_dim(pad_mask, here * frames_own, frames_own, 0) == 1
    patches_own = patches // devices
    keep_cols = lax.dynamic_slice_in_dim(pad_mask, here * patches_own, patches_own, 1) == 1
    space_allowed = keep_own[:, None, :] | jnp.eye(patches, dtype=bool)[None]
    same_clip = segment[:, None] == segment[None, :]
    time_allowed = same_clip[None] & (
        jnp.transpose(keep_cols)[:, None, :] | jnp.eye(frames_all, dtype=bool)[None]
    )
    cond = jax.nn.silu(timestep).astype(jnp.bfloat16)

    def space_in(mixing):
        return attention_forward(mixing, space_allowed, "gx")

    def space_out(state, grad_attended):
        return attention_backward(state, grad_attended, space_allowed, "gx")

    def time_in(mixing):
        moved = lax.all_to_all(mixing, ("wide", "narrow"), split_axis=1, concat_axis=0, tiled=True)
        result, state = attention_forward(moved, time_allowed, "xg")
        return (
            lax.all_to_all(result, ("wide", "narrow"), split_axis=0, concat_axis=1, tiled=True),
            state,
        )

    def time_out(state, grad_attended):
        moved = lax.all_to_all(
            grad_attended, ("wide", "narrow"), split_axis=1, concat_axis=0, tiled=True
        )
        grads = attention_backward(state, moved, time_allowed, "xg")
        return lax.all_to_all(grads, ("wide", "narrow"), split_axis=0, concat_axis=1, tiled=True)

    space_mixer = (space_in, space_out)
    time_mixer = (time_in, time_out)
    space_shards = (
        spacemodulation,
        spaceoffsets,
        spacemixing,
        spaceoutput,
        spaceexpand,
        spacereduce,
    )
    time_shards = (timemodulation, timeoffsets, timemixing, timeoutput, timeexpand, timereduce)
    start = tokens.astype(jnp.float32).reshape(frames_own, patches, width)
    space_full = fetch(space_shards)
    first, space_kept = forward(start, space_full, cond, onehot_own, space_mixer)
    time_full = fetch(time_shards)
    second, time_kept = forward(first, time_full, cond, onehot_own, time_mixer)
    time_back = fetch(time_shards)
    time_kept = forward(first, time_back, cond, onehot_own, time_mixer)[1]
    upstream = cotangent.astype(jnp.float32).reshape(frames_own, patches, width)
    grad_first, time_grads = backward(
        time_kept, time_back, upstream, cond, onehot_own, time_mixer, here, devices
    )
    space_back = fetch(space_shards)
    space_kept = forward(start, space_back, cond, onehot_own, space_mixer)[1]
    grad_start, space_grads = backward(
        space_kept, space_back, grad_first, cond, onehot_own, space_mixer, here, devices
    )
    return (
        first.reshape(-1, width),
        second.reshape(-1, width),
        grad_start.reshape(-1, width),
        space_grads[0],
        space_grads[1],
        space_grads[2],
        space_grads[3],
        space_grads[4],
        space_grads[5],
        time_grads[0],
        time_grads[1],
        time_grads[2],
        time_grads[3],
        time_grads[4],
        time_grads[5],
    )


def solution(mesh):
    return jax.shard_map(
        per_device,
        mesh=mesh,
        in_specs=(
            P(("wide", "narrow"), None),
            P(),
            P(),
            P(),
            P(("wide", "narrow"), None),
            P(("wide", "narrow")),
            P(("wide", "narrow"), None),
            P(("wide", "narrow"), None),
            P(("wide", "narrow"), None),
            P(("wide", "narrow"), None),
            P(("wide", "narrow"), None),
            P(("wide", "narrow")),
            P(("wide", "narrow"), None),
            P(("wide", "narrow"), None),
            P(("wide", "narrow"), None),
            P(("wide", "narrow"), None),
            P(("wide", "narrow"), None),
        ),
        out_specs=(
            P(("wide", "narrow"), None),
            P(("wide", "narrow"), None),
            P(("wide", "narrow"), None),
            P(("wide", "narrow"), None),
            P(("wide", "narrow")),
            P(("wide", "narrow"), None),
            P(("wide", "narrow"), None),
            P(("wide", "narrow"), None),
            P(("wide", "narrow"), None),
            P(("wide", "narrow"), None),
            P(("wide", "narrow")),
            P(("wide", "narrow"), None),
            P(("wide", "narrow"), None),
            P(("wide", "narrow"), None),
            P(("wide", "narrow"), None),
        ),
        check_vma=False,
    )
```

profile of v0, /device:TPU:0, one launch (start us, length us, event | category | flops | bytes accessed | tf_op | source)
XLA Modules:
  0.0 1763.3 jit_solution(10223785109067957971)
XLA Ops:
  21.1 42.5 %all-reduce.3 = (bf16[4608]{0:T(1024)(128)(2,1)S(1)}, bf16[4608]{0:T(1024)(128)(2,1)S(1)}) all-reduce(bf16[4608]{0:T(1024)(128)(2,1)S(1)} %dynamic-update-slice, bf16[4608]{0:T(1024)(128)(2,1)S(1)} %dynamic-update-slice.1), channel_id=1, replica_groups=mesh['wide'=8,'narrow'=4] {'wide','narrow'}, use_global_device_ids=true, to_apply=%add | all-reduce | flops 9216 | bytes 36864
  64.4 22.5 %all-gather.11.cloned.1.call-done = bf16[768,4608]{1,0:T(8,128)(2,1)} async-done(((bf16[24,4608]{1,0:T(8,128)(2,1)}), bf16[768,4608]{1,0:T(8,128)(2,1)}) %all-gather.11.cloned.1.call-update) | async-done | bytes 7077904 | tf_op jit(solution)/shard_map/all_gather | solution.py:192
  86.9 4.0 convolution_add_fusion.1
  92.4 68.4 %all-gather.21.cloned.1.call-done = bf16[768,4608]{1,0:T(8,128)(2,1)} async-done(((bf16[24,4608]{1,0:T(8,128)(2,1)}), bf16[768,4608]{1,0:T(8,128)(2,1)}) %all-gather.21.cloned.1.call-update) | async-done | bytes 7077904 | tf_op jit(solution)/shard_map/all_gather | solution.py:192
  160.9 4.0 convolution_add_fusion
  166.3 56.1 %all-gather.13.cloned.1.call-done = bf16[768,2304]{1,0:T(8,128)(2,1)} async-done(((bf16[24,2304]{1,0:T(8,128)(2,1)}), bf16[768,2304]{1,0:T(8,128)(2,1)}) %all-gather.13.cloned.1.call-update) | async-done | bytes 3538960 | tf_op jit(solution)/shard_map/all_gather | solution.py:194
  232.7 45.4 %all-gather.15.cloned.1.call-done = bf16[768,768]{1,0:T(8,128)(2,1)} async-done(((bf16[24,768]{1,0:T(8,128)(2,1)}), bf16[768,768]{1,0:T(8,128)(2,1)}) %all-gather.15.cloned.1.call-update) | async-done | bytes 1179664 | tf_op jit(solution)/shard_map/all_gather | solution.py:195
  283.1 60.3 %all-gather.17.cloned.1.call-done = bf16[768,3072]{1,0:T(8,128)(2,1)} async-done(((bf16[24,3072]{1,0:T(8,128)(2,1)}), bf16[768,3072]{1,0:T(8,128)(2,1)}) %all-gather.17.cloned.1.call-update) | async-done | bytes 4718608 | tf_op jit(solution)/shard_map/all_gather | solution.py:196
  343.3 5.7 fusion.101
  349.1 59.4 %all-gather.19.cloned.1.call-done = bf16[3072,768]{1,0:T(8,128)(2,1)} async-done(((bf16[96,768]{1,0:T(8,128)(2,1)}), bf16[3072,768]{1,0:T(8,128)(2,1)}) %all-gather.19.cloned.1.call-update) | async-done | bytes 4718608 | tf_op jit(solution)/shard_map/all_gather | solution.py:197
  408.5 6.3 fusion.110
  417.0 53.4 %all-gather.23.cloned.1.call-done = bf16[768,2304]{1,0:T(8,128)(2,1)} async-done(((bf16[24,2304]{1,0:T(8,128)(2,1)}), bf16[768,2304]{1,0:T(8,128)(2,1)}) %all-gather.23.cloned.1.call-update) | async-done | bytes 3538960 | tf_op jit(solution)/shard_map/all_gather | solution.py:194
  477.5 10.3 reduce.94
  487.8 3.9 reshape.865
  491.7 3.5 all-to-all-start
  498.8 30.1 %all-to-all-done = bf16[32,2,9216]{2,1,0:T(2,128)(2,1)} async-done(((bf16[32,2,9216]{2,1,0:T(2,128)(2,1)}), bf16[32,2,9216]{2,1,0:T(2,128)(2,1)}, u32[]{:S(2)}, u32[]{:S(2)}) %all-to-all-start) | async-done | bytes 1179680 | tf_op jit(solution)/shard_map/all_to_all | solution.py:252
  528.9 5.8 reshape.866
  534.8 9.6 bitcast_reduce_fusion
  544.3 4.7 reshape.814
  558.4 3.8 all-to-all-start.1
  562.2 16.3 all-to-all-done.1
  583.8 16.3 all-gather.27.cloned.1.call-done
  600.1 5.7 fusion.103
  605.8 59.4 %all-gather.29.cloned.1.call-done = bf16[3072,768]{1,0:T(8,128)(2,1)} async-done(((bf16[96,768]{1,0:T(8,128)(2,1)}), bf16[3072,768]{1,0:T(8,128)(2,1)}) %all-gather.29.cloned.1.call-update) | async-done | bytes 4718608 | tf_op jit(solution)/shard_map/all_gather | solution.py:197
  665.2 6.2 fusion.14
  677.0 4.7 reduce.95
  683.6 3.7 all-to-all-start.2
  688.8 12.1 all-to-all-done.2
  704.4 4.2 bitcast_reduce_fusion.1
  711.0 3.6 multiply_reduce_fusion.1
  720.7 4.8 convert_element_type.194
  732.8 25.1 %all-to-all-done.3 = bf16[32,8,2304]{2,1,0:T(8,128)(2,1)} async-done(((bf16[32,8,2304]{2,1,0:T(8,128)(2,1)}), bf16[32,8,2304]{2,1,0:T(8,128)(2,1)}, u32[]{:S(2)}, u32[]{:S(2)}) %all-to-all-start.3) | async-done | bytes 1179680 | tf_op jit(solution)/shard_map/all_to_all | solution.py:264
  757.9 4.6 multiply_reduce_fusion.4
  764.5 6.2 fusion.55
  791.7 4.2 fusion.96
  797.0 5.5 fusion.43
  804.4 6.9 fusion.68
  812.9 5.2 fusion.102
  820.1 7.1 fusion.75
  828.8 5.2 fusion.100
  839.5 42.1 %all-reduce.5 = (bf16[4,4608]{1,0:T(4,128)(2,1)S(1)}, bf16[4,4608]{1,0:T(4,128)(2,1)S(1)}) all-reduce(f32[4,4608]{1,0:T(4,128)S(1)} %get-tuple-element.68, f32[4,4608]{1,0:T(4,128)S(1)} %get-tuple-element.67), channel_id=1, replica_groups=mesh['wide'=8,'narrow'=4] {'wide','narrow'}, use_global_device_ids=true, to_apply=%region_30.31 | all-reduce | flops 36864 | bytes 221184 | tf_op jit(solution)/shard_map/psum | solution.py:171
  887.7 52.7 %reduce-scatter.11.cloned.1.call-done = f32[24,768]{1,0:T(8,128)} async-done(((f32[768,768]{1,0:T(8,128)}), f32[24,768]{1,0:T(8,128)}) %reduce-scatter.11.cloned.1.call-update) | async-done | bytes 73744 | tf_op jit(solution)/shard_map/reduce_scatter | solution.py:183
  940.4 124.4 %reduce-scatter.9.cloned.1.call-done = f32[24,2304]{1,0:T(8,128)} async-done(((f32[768,2304]{1,0:T(8,128)}), f32[24,2304]{1,0:T(8,128)}) %reduce-scatter.9.cloned.1.call-update) | async-done | bytes 221200 | tf_op jit(solution)/shard_map/reduce_scatter | solution.py:182
  1064.8 125.4 %reduce-scatter.17.cloned.1.call-done = f32[24,2304]{1,0:T(8,128)} async-done(((f32[768,2304]{1,0:T(8,128)}), f32[24,2304]{1,0:T(8,128)}) %reduce-scatter.17.cloned.1.call-update) | async-done | bytes 221200 | tf_op jit(solution)/shard_map/reduce_scatter | solution.py:182
  1190.2 141.2 %reduce-scatter.23.cloned.1.call-done = f32[96,768]{1,0:T(8,128)} async-done(((f32[3072,768]{1,0:T(8,128)}), f32[96,768]{1,0:T(8,128)}) %reduce-scatter.23.cloned.1.call-update) | async-done | bytes 294928 | tf_op jit(solution)/shard_map/reduce_scatter | solution.py:185
  1331.4 141.9 %reduce-scatter.21.cloned.1.call-done = f32[24,3072]{1,0:T(8,128)} async-done(((f32[768,3072]{1,0:T(8,128)}), f32[24,3072]{1,0:T(8,128)}) %reduce-scatter.21.cloned.1.call-update) | async-done | bytes 294928 | tf_op jit(solution)/shard_map/reduce_scatter | solution.py:184
  1473.3 140.8 %reduce-scatter.15.cloned.1.call-done = f32[96,768]{1,0:T(8,128)} async-done(((f32[3072,768]{1,0:T(8,128)}), f32[96,768]{1,0:T(8,128)}) %reduce-scatter.15.cloned.1.call-update) | async-done | bytes 294928 | tf_op jit(solution)/shard_map/reduce_scatter | solution.py:185
  1614.1 142.2 %reduce-scatter.13.cloned.1.call-done = f32[24,3072]{1,0:T(8,128)} async-done(((f32[768,3072]{1,0:T(8,128)}), f32[24,3072]{1,0:T(8,128)}) %reduce-scatter.13.cloned.1.call-update) | async-done | bytes 294928 | tf_op jit(solution)/shard_map/reduce_scatter | solution.py:184
  (389 shorter events, 130.3 us)
Async XLA Ops:
  7.2 79.7 %all-gather.11.cloned.1.call-start = ((), (), s32[]{:S(2)}) async-start(), calls=%async_computation.12 | async-start | bytes 7299072 | tf_op jit(solution)/shard_map/all_gather | solution.py:192
  7.9 152.9 %all-gather.21.cloned.1.call-start = ((), (), s32[]{:S(2)}) async-start(), calls=%async_computation.17 | async-start | bytes 7299072 | tf_op jit(solution)/shard_map/all_gather | solution.py:192
  8.7 213.8 %all-gather.13.cloned.1.call-start = ((), (), s32[]{:S(2)}) async-start(), calls=%async_computation.13 | async-start | bytes 3649536 | tf_op jit(solution)/shard_map/all_gather | solution.py:194
  9.4 268.7 %all-gather.15.cloned.1.call-start = ((), (), s32[]{:S(2)}) async-start(), calls=%async_computation.14 | async-start | bytes 1216512 | tf_op jit(solution)/shard_map/all_gather | solution.py:195
  10.0 333.4 %all-gather.17.cloned.1.call-start = ((), (), s32[]{:S(2)}) async-start(), calls=%async_computation.15 | async-start | bytes 4866048 | tf_op jit(solution)/shard_map/all_gather | solution.py:196
  10.6 397.9 %all-gather.19.cloned.1.call-start = ((), (), s32[]{:S(2)}) async-start(), calls=%async_computation.16 | async-start | bytes 4866048 | tf_op jit(solution)/shard_map/all_gather | solution.py:197
  11.1 459.2 %all-gather.23.cloned.1.call-start = ((), (), s32[]{:S(2)}) async-start(), calls=%async_computation.18 | async-start | bytes 3649536 | tf_op jit(solution)/shard_map/all_gather | solution.py:194
  11.9 550.3 %all-gather.25.cloned.1.call-start = ((), (), s32[]{:S(2)}) async-start(), calls=%async_computation.19 | async-start | bytes 1216512 | tf_op jit(solution)/shard_map/all_gather | solution.py:195
  12.6 587.4 %all-gather.27.cloned.1.call-start = ((), (), s32[]{:S(2)}) async-start(), calls=%async_computation.20 | async-start | bytes 4866048 | tf_op jit(solution)/shard_map/all_gather | solution.py:196
  13.4 651.8 %all-gather.29.cloned.1.call-start = ((), (), s32[]{:S(2)}) async-start(), calls=%async_computation.21 | async-start | bytes 4866048 | tf_op jit(solution)/shard_map/all_gather | solution.py:197
  17.4 205.1 %copy-start.68 = (f32[256]{0:T(256)}, f32[256]{0:T(256)S(1)}, u32[]{:S(2)}) copy-start(f32[256]{0:T(256)S(1)} %broadcast_multiply_fusion.5) | copy-start | bytes 3076
  18.7 203.8 %copy-start.72 = (f32[256]{0:T(256)}, f32[256]{0:T(256)S(1)}, u32[]{:S(2)}) copy-start(f32[256]{0:T(256)S(1)} %fusion.90) | copy-start | bytes 3076
  19.4 141.4 %copy-start.63 = (bf16[4,768]{1,0:T(4,128)(2,1)}, bf16[4,768]{1,0:T(4,128)(2,1)S(1)}, u32[]{:S(2)}) copy-start(bf16[4,768]{1,0:T(4,128)(2,1)S(1)} %fusion.83) | copy-start | bytes 18436
  92.4 130.0 %copy-start.45 = (f32[768]{0:T(1024)}, f32[768]{0:T(1024)S(1)}, u32[]{:S(2)}) copy-start(f32[768]{0:T(1024)S(1)} %get-tuple-element.39) | copy-start | bytes 9220
  92.4 130.0 %copy-start.58 = (f32[768]{0:T(1024)}, f32[768]{0:T(1024)S(1)}, u32[]{:S(2)}) copy-start(f32[768]{0:T(1024)S(1)} %get-tuple-element.38) | copy-start | bytes 9220
  92.4 250.9 %copy-start.54 = (f32[768]{0:T(1024)}, f32[768]{0:T(1024)S(1)}, u32[]{:S(2)}) copy-start(f32[768]{0:T(1024)S(1)} %get-tuple-element.36) | copy-start | bytes 9220
  92.4 683.7 %copy-start.48 = (f32[768]{0:T(1024)}, f32[768]{0:T(1024)S(1)}, u32[]{:S(2)}) copy-start(f32[768]{0:T(1024)S(1)} %get-tuple-element.37) | copy-start | bytes 9220
  92.4 130.0 %copy-start.2 = (bf16[256,768]{1,0:T(8,128)(2,1)S(1)}, bf16[256,768]{1,0:T(8,128)(2,1)}, u32[]{:S(2)}) copy-start(bf16[256,768]{1,0:T(8,128)(2,1)} %param.17) | copy-start | bytes 1179652
  232.7 441.0 %copy-start.50 = (f32[768]{0:T(1024)}, f32[768]{0:T(1024)S(1)}, u32[]{:S(2)}) copy-start(f32[768]{0:T(1024)S(1)} %get-tuple-element.31) | copy-start | bytes 9220
  232.7 530.6 %copy-start.52 = (f32[768]{0:T(1024)}, f32[768]{0:T(1024)S(1)}, u32[]{:S(2)}) copy-start(f32[768]{0:T(1024)S(1)} %get-tuple-element.33) | copy-start | bytes 9220
  408.5 61.9 %copy-start.60 = (f32[768]{0:T(1024)S(1)}, f32[768]{0:T(1024)}, u32[]{:S(2)}) copy-start(f32[768]{0:T(1024)} %get-tuple-element.32) | copy-start | bytes 9220
  491.7 37.3 %all-to-all-start = ((bf16[32,2,9216]{2,1,0:T(2,128)(2,1)}), bf16[32,2,9216]{2,1,0:T(2,128)(2,1)}, u32[]{:S(2)}, u32[]{:S(2)}) async-start(bf16[32,2,9216]{2,1,0:T(2,128)(2,1)} %reshape.865), calls=%async_computation | async-start | bytes 2359296 | tf_op jit(solution)/shard_map/all_to_all | solution.py:252
  555.8 44.3 %copy-start.56 = (f32[768]{0:T(1024)S(1)}, f32[768]{0:T(1024)}, u32[]{:S(2)}) copy-start(f32[768]{0:T(1024)} %get-tuple-element.30) | copy-start | bytes 9220
  558.4 20.1 %all-to-all-start.1 = ((bf16[32,8,768]{2,1,0:T(8,128)(2,1)}), bf16[32,8,768]{2,1,0:T(8,128)(2,1)}, u32[]{:S(2)}, u32[]{:S(2)}) async-start(bf16[32,8,768]{2,1,0:T(8,128)(2,1)} %reshape.815), calls=%async_computation.1 | async-start | bytes 786432 | tf_op jit(solution)/shard_map/all_to_all | solution.py:255
  665.2 6.3 copy-start.92
  665.2 6.3 copy-start.112
  674.1 9.5 copy-start.94
  683.6 17.4 all-to-all-start.2
  725.4 32.5 %all-to-all-start.3 = ((bf16[32,8,2304]{2,1,0:T(8,128)(2,1)}), bf16[32,8,2304]{2,1,0:T(8,128)(2,1)}, u32[]{:S(2)}, u32[]{:S(2)}) async-start(bf16[32,8,2304]{2,1,0:T(8,128)(2,1)} %convert_element_type.194), calls=%async_computation.3 | async-start | bytes 2359296 | tf_op jit(solution)/shard_map/all_to_all | solution.py:264
  728.8 29.1 %copy-start.79 = (f32[256]{0:T(256)S(1)}, f32[256]{0:T(256)}, u32[]{:S(2)}) copy-start(f32[256]{0:T(256)} %copy-done.78) | copy-start | bytes 3076
  728.8 158.8 %reduce-scatter.19.cloned.1.call-start = ((), (), s32[]{:S(2)}) async-start(), calls=%async_computation.27 | async-start | bytes 2433024 | tf_op jit(solution)/shard_map/reduce_scatter | solution.py:183
  732.3 32.1 %copy-start.87 = (f32[768]{0:T(1024)S(1)}, f32[768]{0:T(1024)}, u32[]{:S(2)}) copy-start(f32[768]{0:T(1024)} %get-tuple-element.29) | copy-start | bytes 9220
  732.3 208.1 %reduce-scatter.11.cloned.1.call-start = ((), (), s32[]{:S(2)}) async-start(), calls=%async_computation.23 | async-start | bytes 2433024 | tf_op jit(solution)/shard_map/reduce_scatter | solution.py:183
  757.9 6.5 copy-start.13
  757.9 6.5 copy-start.16
  757.9 6.5 copy-start.20
  757.9 6.5 copy-start.27
  757.9 6.5 copy-start.42
  757.9 6.5 copy-start.113
  763.3 7.4 slice-start.2
  764.5 9.3 slice-start
  780.1 284.7 %reduce-scatter.9.cloned.1.call-start = ((), (), s32[]{:S(2)}) async-start(), calls=%async_computation.22 | async-start | bytes 7299072 | tf_op jit(solution)/shard_map/reduce_scatter | solution.py:182
  795.9 394.3 %reduce-scatter.17.cloned.1.call-start = ((), (), s32[]{:S(2)}) async-start(), calls=%async_computation.26 | async-start | bytes 7299072 | tf_op jit(solution)/shard_map/reduce_scatter | solution.py:182
  802.5 528.9 %reduce-scatter.23.cloned.1.call-start = ((), (), s32[]{:S(2)}) async-start(), calls=%async_computation.29 | async-start | bytes 9732096 | tf_op jit(solution)/shard_map/reduce_scatter | solution.py:185
  811.3 662.0 %reduce-scatter.21.cloned.1.call-start = ((), (), s32[]{:S(2)}) async-start(), calls=%async_computation.28 | async-start | bytes 9732096 | tf_op jit(solution)/shard_map/reduce_scatter | solution.py:184
  818.2 795.9 %reduce-scatter.15.cloned.1.call-start = ((), (), s32[]{:S(2)}) async-start(), calls=%async_computation.25 | async-start | bytes 9732096 | tf_op jit(solution)/shard_map/reduce_scatter | solution.py:185
  827.2 929.1 %reduce-scatter.13.cloned.1.call-start = ((), (), s32[]{:S(2)}) async-start(), calls=%async_computation.24 | async-start | bytes 9732096 | tf_op jit(solution)/shard_map/reduce_scatter | solution.py:184
  835.4 51.1 %copy-start.7 = (f32[256,768]{1,0:T(8,128)S(1)}, f32[256,768]{1,0:T(8,128)}, u32[]{:S(2)}) copy-start(f32[256,768]{1,0:T(8,128)} %copy-done.6) | copy-start | bytes 2359300
  (92 other events, 201.3 us)
Sparse Core Ops, SparseCore 0:
  10.9 75.9 all-gather.10
  89.8 71.0 all-gather.20
  163.7 58.6 all-gather.12
  225.2 52.8 all-gather.14
  280.8 62.4 all-gather.16
  346.1 62.3 all-gather.18
  411.4 58.9 all-gather.22
  473.2 56.8 all-gather.24
  533.1 66.9 all-gather.26
  602.8 62.3 all-gather.28
  735.5 100.1 reduce-scatter.18
  842.3 98.0 reduce-scatter.10
  946.6 118.1 reduce-scatter.8
  1071.9 118.3 reduce-scatter.16
  1196.6 134.8 reduce-scatter.22
  1338.8 134.4 reduce-scatter.20
  1479.6 134.4 reduce-scatter.14
  1621.4 134.8 reduce-scatter.12
where the time goes:
time: 1770 us; the launch traced here: 1760 us
  waiting for transfers between devices  1400 us (79%)
  matrix products  130 us (7%)
  blocking collectives  84.6 us (5%)
  local copies, waits for them, and re-layouts  79.5 us (4%)
  other arithmetic  38.1 us (2%)
    reduce_scatter x2, waiting for transfers between devices, backward(): lax.psum_scatter(grad_up, ('wide', 'narrow'), scatter_dimension=0, tiled=...  284 us
    reduce_scatter x2, waiting for transfers between devices, backward(): lax.psum_scatter(grad_down, ('wide', 'narrow'), scatter_dimension=0, tile...  282 us
    reduce_scatter x2, waiting for transfers between devices, backward(): lax.psum_scatter(grad_project, ('wide', 'narrow'), scatter_dimension=0, t...  250 us
    all_gather x2, waiting for transfers between devices, fetch(): lax.all_gather(shards[5], ('wide', 'narrow'), axis=0, tiled=True)  119 us
    all_gather x2, waiting for transfers between devices, fetch(): lax.all_gather(shards[2], ('wide', 'narrow'), axis=0, tiled=True)  109 us
    all_gather x2, waiting for transfers between devices, fetch(): lax.all_gather(shards[0], ('wide', 'narrow'), axis=0, tiled=True)  90.9 us
    all_gather x2, waiting for transfers between devices, fetch(): lax.all_gather(shards[4], ('wide', 'narrow'), axis=0, tiled=True)  76.5 us
    reduce_scatter x2, waiting for transfers between devices, backward(): lax.psum_scatter(grad_output, ('wide', 'narrow'), scatter_dimension=0, ti...  52.7 us
  transfers between devices with their start and end apart: 22, of which 20 were waited for; matrix products, arithmetic and copies ran while one was open for 11% of the time, Pallas kernels for 0%

commit v1 on v0

--- a/solution.py
+++ b/solution.py
@@ -116,9 +116,8 @@
     return stacked.reshape(mixing.shape).astype(jnp.bfloat16)
 
 
-def forward(inputs, weights, cond, onehot_own, mixer):
-    w_mod, w_bias, w_mix, w_out, w_up, w_down = weights
-    table = jnp.dot(cond, w_mod, preferred_element_type=jnp.float32) + w_bias.astype(jnp.float32)
+def forward(inputs, weights, table, onehot_own, mixer):
+    w_mix, w_out, w_up, w_down = weights
     mods = jnp.dot(onehot_own, table, precision=lax.Precision.HIGHEST)[:, None, :]
     pieces = jnp.split(mods, 6, axis=2)
     normed = modulate(inputs, pieces[1], pieces[0]).astype(jnp.bfloat16)
@@ -137,9 +136,9 @@
     )
 
 
-def backward(kept, weights, grad, cond, onehot_own, mixer, here, devices):
+def backward(kept, weights, grad, onehot_own, mixer):
     inputs, pieces, normed, state, attended, branch, middle, normed_b, hidden, active, out = kept
-    w_mod, w_bias, w_mix, w_out, w_up, w_down = weights
+    w_mix, w_out, w_up, w_down = weights
     grad_out = (pieces[5] * grad).astype(jnp.bfloat16)
     grad_gate_b = jnp.sum(out * grad, axis=1, keepdims=True)
     grad_down = outer(active, grad_out)
@@ -168,34 +167,56 @@
     grad_table = lax.dot_general(
         onehot_own, grad_frames, (((0,), (0,)), ((), ())), precision=lax.Precision.HIGHEST
     )
-    summed = lax.psum(grad_table, ("wide", "narrow")).astype(jnp.bfloat16)
-    row_count = w_mod.shape[0] // devices
+    return (grad_input, grad_table, (grad_project, grad_output, grad_up, grad_down))
+
+
+def partial_table(cond, w_mod, w_bias, here):
+    row_count = w_mod.shape[0]
+    cond_rows = lax.dynamic_slice_in_dim(cond, here * row_count, row_count, 1)
+    table = jnp.dot(cond_rows, w_mod, preferred_element_type=jnp.float32)
+    bias = lax.dynamic_update_slice_in_dim(
+        jnp.zeros((w_mod.shape[1],), jnp.float32),
+        w_bias.astype(jnp.float32),
+        here * w_bias.shape[0],
+        0,
+    )
+    return table + bias[None]
+
+
+def modulation_grads(summed, cond, w_mod, w_bias, here):
+    row_count, bias_count = w_mod.shape[0], w_bias.shape[0]
     cond_rows = lax.dynamic_slice_in_dim(cond, here * row_count, row_count, 1)
     grad_mod = lax.dot_general(
         cond_rows, summed, (((0,), (0,)), ((), ())), preferred_element_type=jnp.float32
     )
-    bias_count = w_bias.shape[0] // devices
     grad_bias = lax.dynamic_slice_in_dim(
         jnp.sum(summed.astype(jnp.float32), axis=0), here * bias_count, bias_count, 0
     )
-    owned = (
-        lax.psum_scatter(grad_project, ("wide", "narrow"), scatter_dimension=0, tiled=True),
-        lax.psum_scatter(grad_output, ("wide", "narrow"), scatter_dimension=0, tiled=True),
-        lax.psum_scatter(grad_up, ("wide", "narrow"), scatter_dimension=0, tiled=True),
-        lax.psum_scatter(grad_down, ("wide", "narrow"), scatter_dimension=0, tiled=True),
-    )
-    return (grad_input, (grad_mod, grad_bias, owned[0], owned[1], owned[2], owned[3]))
+    return grad_mod, grad_bias
 
 
 def fetch(shards):
-    return (
-        lax.all_gather(shards[0], ("wide", "narrow"), axis=0, tiled=True),
-        lax.all_gather(shards[1], ("wide", "narrow"), axis=0, tiled=True),
-        lax.all_gather(shards[2], ("wide", "narrow"), axis=0, tiled=True),
-        lax.all_gather(shards[3], ("wide", "narrow"), axis=0, tiled=True),
-        lax.all_gather(shards[4], ("wide", "narrow"), axis=0, tiled=True),
-        lax.all_gather(shards[5], ("wide", "narrow"), axis=0, tiled=True),
-    )
+    rows = shards[0].shape[0]
+    packed = jnp.concatenate([part.reshape(rows, -1) for part in shards], axis=1)
+    full = lax.all_gather(packed, ("wide", "narrow"), axis=0, tiled=True)
+    out, at = [], 0
+    for part in shards:
+        wide = part.size // rows
+        out.append(full[:, at : at + wide].reshape(-1, part.shape[1]))
+        at += wide
+    return tuple(out)
+
+
+def scatter(grads):
+    rows = grads[0].shape[0]
+    packed = jnp.concatenate([g.astype(jnp.bfloat16).reshape(rows, -1) for g in grads], axis=1)
+    own = lax.psum_scatter(packed, ("wide", "narrow"), scatter_dimension=0, tiled=True)
+    out, at = [], 0
+    for g in grads:
+        wide = g.size // rows
+        out.append(own[:, at : at + wide].reshape(-1, g.shape[1]).astype(jnp.float32))
+        at += wide
+    return out
 
 
 def per_device(
@@ -265,30 +286,44 @@
 
     space_mixer = (space_in, space_out)
     time_mixer = (time_in, time_out)
-    space_shards = (
-        spacemodulation,
-        spaceoffsets,
-        spacemixing,
-        spaceoutput,
-        spaceexpand,
-        spacereduce,
-    )
-    time_shards = (timemodulation, timeoffsets, timemixing, timeoutput, timeexpand, timereduce)
+    space_shards = (spacemixing, spaceoutput, spaceexpand, spacereduce)
+    time_shards = (timemixing, timeoutput, timeexpand, timereduce)
+    tables = lax.psum(
+        jnp.concatenate(
+            [
+                partial_table(cond, spacemodulation, spaceoffsets, here),
+                partial_table(cond, timemodulation, timeoffsets, here),
+            ],
+            axis=0,
+        ),
+        ("wide", "narrow"),
+    )
+    clips = clip_lengths.shape[0]
+    space_table, time_table = tables[:clips], tables[clips:]
     start = tokens.astype(jnp.float32).reshape(frames_own, patches, width)
     space_full = fetch(space_shards)
-    first, space_kept = forward(start, space_full, cond, onehot_own, space_mixer)
     time_full = fetch(time_shards)
-    second, time_kept = forward(first, time_full, cond, onehot_own, time_mixer)
-    time_back = fetch(time_shards)
-    time_kept = forward(first, time_back, cond, onehot_own, time_mixer)[1]
+    first, space_kept = forward(start, space_full, space_table, onehot_own, space_mixer)
+    second, time_kept = forward(first, time_full, time_table, onehot_own, time_mixer)
     upstream = cotangent.astype(jnp.float32).reshape(frames_own, patches, width)
-    grad_first, time_grads = backward(
-        time_kept, time_back, upstream, cond, onehot_own, time_mixer, here, devices
-    )
-    space_back = fetch(space_shards)
-    space_kept = forward(start, space_back, cond, onehot_own, space_mixer)[1]
-    grad_start, space_grads = backward(
-        space_kept, space_back, grad_first, cond, onehot_own, space_mixer, here, devices
+    grad_first, time_frames, time_raw = backward(
+        time_kept, time_full, upstream, onehot_own, time_mixer
+    )
+    time_own = scatter(time_raw)
+    grad_start, space_frames, space_raw = backward(
+        space_kept, space_full, grad_first, onehot_own, space_mixer
+    )
+    space_own = scatter(space_raw)
+    summed = lax.psum(
+        jnp.concatenate([space_frames, time_frames], axis=0), ("wide", "narrow")
+    ).astype(jnp.bfloat16)
+    space_grads = (
+        *modulation_grads(summed[:clips], cond, spacemodulation, spaceoffsets, here),
+        *space_own,
+    )
+    time_grads = (
+        *modulation_grads(summed[clips:], cond, timemodulation, timeoffsets, here),
+        *time_own,
     )
     return (
         first.reshape(-1, width),

time: 1770 us -> 974 us (0.55)
  waiting for transfers between devices: 1400 us -> 600 us
  local copies, waits for them, and re-layouts: 79.5 us -> 122 us
  blocking collectives: 84.6 us -> 44.6 us
  other arithmetic: 38.1 us -> 61.2 us
  matrix products: 130 us -> 109 us
    reduce_scatter x8 -> x2, waiting for transfers between devices: 869 us -> 234 us  [scatter(): lax.psum_scatter(packed, ('wide', 'narrow'), scatter_dimension=0, tiled=T...]
    all_gather x10 -> x2, waiting for transfers between devices: 441 us -> 176 us  [fetch(): full = lax.all_gather(packed, ('wide', 'narrow'), axis=0, tiled=True)]
    psum x0 -> x1, waiting for transfers between devices: none -> 118 us  [per_device(): lax.psum(jnp.concatenate([partial_table(cond, spacemodulation, spaceoffse...]
    unnamed x1 -> x0, blocking collectives: 42.5 us -> none
    reshape x0 -> x6, local copies, waits for them, and re-layouts: none -> 36.8 us  [the longest x2 17.4 us: fetch(): out.append(full[:, at:at + wide].reshape(-1, part.shape[1]))]
    concatenate x0 -> x6, other arithmetic: none -> 23 us  [the longest x2 18.9 us: scatter(): jnp.concatenate([g.astype(jnp.bfloat16).reshape(rows, -1) for g in grads]...]
  transfers between devices with their start and end apart: 22 -> 9, of which waited for: 20 -> 9; matrix products, arithmetic and copies ran while one was open for 11% -> 11% of each run, Pallas kernels for 0% -> 0%
where the time goes in v1:
time: 974 us; the launch traced here: 967 us
  waiting for transfers between devices  600 us (62%)
  local copies, waits for them, and re-layouts  122 us (13%)
  matrix products  109 us (11%)
  other arithmetic  61.2 us (6%)
  blocking collectives  44.6 us (5%)
  starting transfers between devices  16.3 us (2%)
  between operations  15.1 us (2%)
    reduce_scatter x2, waiting for transfers between devices, scatter(): lax.psum_scatter(packed, ('wide', 'narrow'), scatter_dimension=0, tiled=T...  234 us
    all_gather x2, waiting for transfers between devices, fetch(): full = lax.all_gather(packed, ('wide', 'narrow'), axis=0, tiled=True)  176 us
    psum x1, waiting for transfers between devices, per_device(): lax.psum(jnp.concatenate([partial_table(cond, spacemodulation, spaceoffse...  118 us
    psum x1, blocking collectives, per_device(): lax.psum(jnp.concatenate([space_frames, time_frames], axis=0), ('wide', '...  44.6 us
    all_to_all x1, waiting for transfers between devices, time_out(): lax.all_to_all(grads, ('wide', 'narrow'), split_axis=0, concat_axis=1, ti...  29 us
    all_to_all x1, waiting for transfers between devices, time_in(): lax.all_to_all(mixing, ('wide', 'narrow'), split_axis=1, concat_axis=0, t...  28.7 us
    dot_general x8, matrix products, against(): lax.dot_general(left, weight, (((left.ndim - 1,), (1,)), ((), ())), prefe...  27.5 us
    dot_general x8, matrix products, outer(): jnp.einsum('fpa,fpb->ab', left, right, preferred_element_type=jnp.float32)  26.5 us
  transfers between devices with their start and end apart: 9, of which 9 were waited for; matrix products, arithmetic and copies ran while one was open for 11% of the time, Pallas kernels for 0%

profile of v1, /device:TPU:0, one launch (start us, length us, event | category | flops | bytes accessed | tf_op | source)
XLA Modules:
  0.0 967.5 jit_solution(547195559371147949)
XLA Ops:
  19.5 118.1 %all-reduce.3.cloned.1.call-done = f32[8,4608]{1,0:T(8,128)} async-done(((f32[8,4608]{1,0:T(8,128)}), f32[8,4608]{1,0:T(8,128)}) %all-reduce.3.cloned.1.call-update) | async-done | bytes 147472 | tf_op jit(solution)/shard_map/psum | solution.py:291
  141.2 105.0 %all-gather.3.cloned.1.call-done = bf16[768,9216]{1,0:T(8,128)(2,1)} async-done(((bf16[24,9216]{1,0:T(8,128)(2,1)}), bf16[768,9216]{1,0:T(8,128)(2,1)}) %all-gather.3.cloned.1.call-update) | async-done | bytes 14155792 | tf_op jit(solution)/shard_map/all_gather | solution.py:201
  246.2 3.2 convolution_convert_fusion.7
  250.9 4.9 slice.117
  255.7 9.0 reshape.843
  271.8 4.2 fusion.6
  276.1 3.1 fusion.124
  280.6 70.5 %all-gather.5.cloned.1.call-done = bf16[768,9216]{1,0:T(8,128)(2,1)} async-done(((bf16[24,9216]{1,0:T(8,128)(2,1)}), bf16[768,9216]{1,0:T(8,128)(2,1)}) %all-gather.5.cloned.1.call-update) | async-done | bytes 14155792 | tf_op jit(solution)/shard_map/all_gather | solution.py:201
  351.1 3.4 fusion.8
  354.5 3.2 copy.141
  358.2 10.0 %reduce.94 = bf16[256,2304]{1,0:T(8,128)(2,1)} reduce(bf16[256,1,2304]{2,1,0:T(2,128)(2,1)} %bitcast.144, bf16[]{:T(256)} %broadcast.502), dimensions={1}, to_apply=%bitcast.138.reduce_sub_computation | reduce | bytes 2359298
  368.2 3.9 reshape.897
  372.1 3.4 all-to-all-start
  375.9 28.7 %all-to-all-done = bf16[32,2,9216]{2,1,0:T(2,128)(2,1)} async-done(((bf16[32,2,9216]{2,1,0:T(2,128)(2,1)}), bf16[32,2,9216]{2,1,0:T(2,128)(2,1)}, u32[]{:S(2)}, u32[]{:S(2)}) %all-to-all-start) | async-done | bytes 1179680 | tf_op jit(solution)/shard_map/all_to_all | solution.py:273
  404.6 5.8 reshape.898
  410.4 9.6 bitcast_reduce_fusion
  419.9 4.7 reshape.845
  434.2 3.6 all-to-all-start.1
  437.9 4.8 slice.125
  442.7 8.5 reshape.848
  451.5 3.0 fusion.123
  454.7 4.2 fusion.2
  461.9 4.5 multiply_reduce_fusion.2
  471.0 4.7 reduce.95
  477.6 5.7 all-to-all-start.2
  483.4 13.6 %all-to-all-done.2 = bf16[32,2,3072]{2,1,0:T(2,128)(2,1)} async-done(((bf16[32,2,3072]{2,1,0:T(2,128)(2,1)}), bf16[32,2,3072]{2,1,0:T(2,128)(2,1)}, u32[]{:S(2)}, u32[]{:S(2)}) %all-to-all-start.2) | async-done | bytes 393248 | tf_op jit(solution)/shard_map/all_to_all | solution.py:281
  496.9 3.4 reshape.900
  500.4 4.2 bitcast_reduce_fusion.1
  517.8 4.7 convert_element_type.231
  522.6 3.4 all-to-all-start.3
  526.0 29.0 %all-to-all-done.3 = bf16[32,8,2304]{2,1,0:T(8,128)(2,1)} async-done(((bf16[32,8,2304]{2,1,0:T(8,128)(2,1)}), bf16[32,8,2304]{2,1,0:T(8,128)(2,1)}, u32[]{:S(2)}, u32[]{:S(2)}) %all-to-all-start.3) | async-done | bytes 1179680 | tf_op jit(solution)/shard_map/all_to_all | solution.py:285
  555.1 4.0 multiply_reduce_fusion.4
  561.4 5.6 fusion.73
  567.0 3.3 fusion.15
  570.3 4.5 multiply_reduce_fusion.6
  587.1 4.4 convolution_convert_fusion.3
  591.5 3.7 convolution_convert_fusion.4
  596.8 8.5 reshape.862
  612.3 9.6 pad_maximum_fusion
  622.9 6.4 convolution_convert_fusion
  629.3 8.8 reshape.863
  643.4 3.2 convolution_convert_fusion.1
  646.6 3.0 convolution_convert_fusion.2
  649.7 9.4 pad_maximum_fusion.1
  659.8 3.9 fusion.71
  664.6 44.6 %all-reduce.4 = bf16[8,4608]{1,0:T(8,128)(2,1)S(1)} all-reduce(f32[8,4608]{1,0:T(8,128)S(1)} %pad_maximum_fusion.7), channel_id=1, replica_groups=mesh['wide'=8,'narrow'=4] {'wide','narrow'}, use_global_device_ids=true, to_apply=%region_37.38 | all-reduce | flops 36864 | bytes 221184 | tf_op jit(solution)/shard_map/psum | solution.py:317
  715.3 69.4 %reduce-scatter.3.cloned.1.call-done = bf16[24,9216]{1,0:T(8,128)(2,1)} async-done(((bf16[768,9216]{1,0:T(8,128)(2,1)}), bf16[24,9216]{1,0:T(8,128)(2,1)}) %reduce-scatter.3.cloned.1.call-update) | async-done | bytes 442384 | tf_op jit(solution)/shard_map/reduce_scatter | solution.py:213
  787.3 164.9 %reduce-scatter.5.cloned.1.call-done = bf16[24,9216]{1,0:T(8,128)(2,1)} async-done(((bf16[768,9216]{1,0:T(8,128)(2,1)}), bf16[24,9216]{1,0:T(8,128)(2,1)}) %reduce-scatter.5.cloned.1.call-update) | async-done | bytes 442384 | tf_op jit(solution)/shard_map/reduce_scatter | solution.py:213
  (260 shorter events, 107.2 us)
Async XLA Ops:
  7.2 8.6 copy-start.42
  7.2 8.6 copy-start.43
  7.2 10.2 %copy-start.45 = (s32[4]{0:T(128)S(1)}, s32[4]{0:T(128)}, u32[]{:S(2)}) copy-start(s32[4]{0:T(128)} %param.19) | copy-start | bytes 52
  7.2 11.8 %copy-start.5 = (bf16[256,768]{1,0:T(8,128)(2,1)S(1)}, bf16[256,768]{1,0:T(8,128)(2,1)}, u32[]{:S(2)}) copy-start(bf16[256,768]{1,0:T(8,128)(2,1)} %param.17) | copy-start | bytes 1179652
  7.2 130.3 %all-reduce.3.cloned.1.call-start = ((), (), s32[]{:S(2)}) async-start(), calls=%async_computation.6 | async-start | bytes 294912 | tf_op jit(solution)/shard_map/psum | solution.py:291
  11.9 234.4 %all-gather.3.cloned.1.call-start = ((), (), s32[]{:S(2)}) async-start(), calls=%async_computation.7 | async-start | bytes 14598144 | tf_op jit(solution)/shard_map/all_gather | solution.py:201
  14.8 336.3 %all-gather.5.cloned.1.call-start = ((), (), s32[]{:S(2)}) async-start(), calls=%async_computation.8 | async-start | bytes 14598144 | tf_op jit(solution)/shard_map/all_gather | solution.py:201
  271.5 4.5 copy-start.8
  271.6 4.5 slice-start.4
  271.8 4.3 slice-start.5
  276.0 3.2 copy-start.46
  368.2 7.3 copy-start.44
  372.1 32.5 %all-to-all-start = ((bf16[32,2,9216]{2,1,0:T(2,128)(2,1)}), bf16[32,2,9216]{2,1,0:T(2,128)(2,1)}, u32[]{:S(2)}, u32[]{:S(2)}) async-start(bf16[32,2,9216]{2,1,0:T(2,128)(2,1)} %reshape.897), calls=%async_computation | async-start | bytes 2359296 | tf_op jit(solution)/shard_map/all_to_all | solution.py:273
  434.2 17.2 %all-to-all-start.1 = ((bf16[32,8,768]{2,1,0:T(8,128)(2,1)}), bf16[32,8,768]{2,1,0:T(8,128)(2,1)}, u32[]{:S(2)}, u32[]{:S(2)}) async-start(bf16[32,8,768]{2,1,0:T(8,128)(2,1)} %reshape.846), calls=%async_computation.1 | async-start | bytes 786432 | tf_op jit(solution)/shard_map/all_to_all | solution.py:276
  454.5 12.0 %copy-start.11 = (f32[256,768]{1,0:T(8,128)}, f32[256,768]{1,0:T(8,128)S(1)}, u32[]{:S(2)}) copy-start(f32[256,768]{1,0:T(8,128)S(1)} %get-tuple-element.54) | copy-start | bytes 2359300
  454.5 4.5 slice-start.8
  454.7 4.3 slice-start.9
  454.7 4.3 copy-start.39
  461.9 4.5 copy-start.32
  477.6 19.3 %all-to-all-start.2 = ((bf16[32,2,3072]{2,1,0:T(2,128)(2,1)}), bf16[32,2,3072]{2,1,0:T(2,128)(2,1)}, u32[]{:S(2)}, u32[]{:S(2)}) async-start(bf16[32,2,3072]{2,1,0:T(2,128)(2,1)} %reshape.899), calls=%async_computation.2 | async-start | bytes 786432 | tf_op jit(solution)/shard_map/all_to_all | solution.py:281
  522.6 32.5 %all-to-all-start.3 = ((bf16[32,8,2304]{2,1,0:T(8,128)(2,1)}), bf16[32,8,2304]{2,1,0:T(8,128)(2,1)}, u32[]{:S(2)}, u32[]{:S(2)}) async-start(bf16[32,8,2304]{2,1,0:T(8,128)(2,1)} %convert_element_type.231), calls=%async_computation.3 | async-start | bytes 2359296 | tf_op jit(solution)/shard_map/all_to_all | solution.py:285
  526.0 258.8 %reduce-scatter.3.cloned.1.call-start = ((), (), s32[]{:S(2)}) async-start(), calls=%async_computation.9 | async-start | bytes 14598144 | tf_op jit(solution)/shard_map/reduce_scatter | solution.py:213
  555.0 6.3 copy-start.12
  555.0 6.3 copy-start.28
  555.0 6.3 copy-start.36
  555.0 6.3 copy-start.40
  555.0 6.3 copy-start.50
  555.0 6.3 copy-start.51
  555.1 11.9 %slice-start.6 = ((s8[4718592]{0:T(1024)(128)(4,1)}), s8[4194304]{0:T(1024)(128)(4,1)S(1)}, s32[]{:S(2)}) async-start(s8[4718592]{0:T(1024)(128)(4,1)} %bitcast.154), calls=%async_computation.17 | async-start | bytes 8388608
  561.4 5.6 slice-start.7
  561.4 5.6 copy-start.47
  566.9 8.3 copy-start.37
  566.9 3.4 copy-start.9
  570.3 4.6 copy-start.33
  570.3 4.9 copy-start.26
  587.1 4.5 copy-start.10
  587.1 4.5 copy-start.34
  591.5 3.7 copy-start.15
  591.5 3.7 copy-start.31
  596.8 11.1 %copy-start.35 = (bf16[1,256,1,12,64]{1,4,3,2,0:T(8,128)(2,1)S(1)}, bf16[1,256,1,12,64]{1,4,3,2,0:T(8,128)(2,1)}, u32[]{:S(2)}) copy-start(bf16[1,256,1,12,64]{1,4,3,2,0:T(8,128)(2,1)} %fusion.49) | copy-start | bytes 1179652
  605.4 3.8 copy-start.7
  609.1 3.2 copy-start.4
  621.9 330.3 %reduce-scatter.5.cloned.1.call-start = ((), (), s32[]{:S(2)}) async-start(), calls=%async_computation.10 | async-start | bytes 14598144 | tf_op jit(solution)/shard_map/reduce_scatter | solution.py:213
  629.3 8.8 copy-start.29
  638.1 5.3 copy-start.13
  640.9 8.7 slice-start.2
  643.4 6.3 slice-start.3
  712.3 248.4 %copy-start.1 = (bf16[24,4608]{1,0:T(8,128)(2,1)S(1)}, bf16[24,4608]{1,0:T(8,128)(2,1)}, u32[]{:S(2)}) copy-start(bf16[24,4608]{1,0:T(8,128)(2,1)} %param.27) | copy-start | bytes 663556
  (23 other events, 46.6 us)
Sparse Core Ops, SparseCore 0:
  14.2 123.3 all-reduce.2
  141.1 105.1 all-gather.2
  249.7 101.3 all-gather.4
  622.0 162.6 reduce-scatter.2
  790.6 161.5 reduce-scatter.4

commit v2 on v1

--- a/solution.py
+++ b/solution.py
@@ -1,6 +1,10 @@
+import functools
+
 import jax
 import jax.numpy as jnp
 from jax import lax
+from jax.experimental import pallas as pl
+from jax.experimental.pallas import tpu as pltpu
 from jax.sharding import PartitionSpec as P
 
 HEADS = 12
@@ -217,6 +221,249 @@
         out.append(own[:, at : at + wide].reshape(-1, g.shape[1]).astype(jnp.float32))
         at += wide
     return out
+
+
+MESH = pl.DeviceIdType.MESH
+BF, F32 = jnp.bfloat16, jnp.float32
+
+def place():
+    w, n = lax.axis_index("wide"), lax.axis_index("narrow")
+    return w // 2, lax.rem(w, 2), n // 2, lax.rem(n, 2)
+
+
+class Gather:
+    def __init__(self, src, out, sems, cut):
+        self.src, self.out, self.sems, self.cut = src, out, sems, cut
+        self.z, self.c, self.y, self.x = place()
+        self.n = 2 * self.y + self.x
+        self.ny, self.nx = 2 * (1 - self.y) + self.x, 2 * self.y + 1 - self.x
+        self.far = 3 - self.n
+
+    def column(self, p, c, n, h):
+        rows, _, cols = self.out.shape[-3:]
+        if self.cut == "cols":
+            return self.out.at[p, :, c, n, :, :, pl.ds(h * (cols // 2), cols // 2)]
+        return self.out.at[p, :, c, n, pl.ds(h * (rows // 2), rows // 2)]
+
+    def block(self, p, z, c, n, h):
+        rows, _, cols = self.out.shape[-3:]
+        if self.cut == "cols":
+            return self.out.at[p, z, c, n, :, :, pl.ds(h * (cols // 2), cols // 2)]
+        return self.out.at[p, z, c, n, pl.ds(h * (rows // 2), rows // 2)]
+
+    def own(self, p, h):
+        rows, _, cols = self.out.shape[-3:]
+        if self.cut == "cols":
+            return self.src.at[p, :, :, pl.ds(h * (cols // 2), cols // 2)]
+        return self.src.at[p, pl.ds(h * (rows // 2), rows // 2)]
+
+    def copy(self, src, dst, p, h, kind, to):
+        recv, send, _ = self.sems
+        return pltpu.make_async_remote_copy(
+            src_ref=src, dst_ref=dst, send_sem=send.at[kind], recv_sem=recv.at[p, h, kind],
+            device_id=to, device_id_type=MESH,
+        )
+
+    def arrived(self, ref, p, h, kind):
+        recv = self.sems[0]
+        pltpu.make_async_copy(ref, ref, recv.at[p, h, kind]).wait()
+
+    def dev(self, z, c, n):
+        return (2 * z + c, n)
+
+    def near(self, h):
+        return (self.ny, self.nx) if h == 0 else (self.nx, self.ny)
+
+    def s0(self, p):
+        for h in range(2):
+            for k in (1, 2, 3):
+                zz = lax.rem(self.z + k, 4)
+                self.copy(self.own(p, h), self.block(p, self.z, self.c, self.n, h), p, h, k - 1, self.dev(zz, self.c, self.n)).start()
+
+    def s1(self, p):
+        for h in range(2):
+            n1, n2 = self.near(h)
+            for k in (1, 2, 3):
+                zz = lax.rem(self.z + 4 - k, 4)
+                self.arrived(self.block(p, zz, self.c, self.n, h), p, h, k - 1)
+            col = self.column(p, self.c, self.n, h)
+            self.copy(col, col, p, h, 3, self.dev(self.z, self.c, n1)).start()
+            self.copy(col, col, p, h, 4, self.dev(self.z, self.c, n2)).start()
+            self.copy(col, col, p, h, 6, self.dev(self.z, 1 - self.c, self.n)).start()
+
+    def s2(self, p):
+        for h in range(2):
+            n1, n2 = self.near(h)
+            col = self.column(p, self.c, n1, h)
+            self.arrived(col, p, h, 3)
+            self.copy(col, col, p, h, 5, self.dev(self.z, self.c, n2)).start()
+            self.copy(col, col, p, h, 7, self.dev(self.z, 1 - self.c, self.n)).start()
+
+    def s3(self, p):
+        for h in range(2):
+            n1, n2 = self.near(h)
+            col = self.column(p, self.c, n2, h)
+            self.arrived(col, p, h, 4)
+            self.copy(col, col, p, h, 8, self.dev(self.z, 1 - self.c, self.n)).start()
+            col = self.column(p, self.c, self.far, h)
+            self.arrived(col, p, h, 5)
+            self.copy(col, col, p, h, 9, self.dev(self.z, 1 - self.c, self.n)).start()
+
+    def s4(self, p):
+        for h in range(2):
+            n1, n2 = self.near(h)
+            for kind, n in ((6, self.n), (7, n1), (8, n2), (9, self.far)):
+                self.arrived(self.column(p, 1 - self.c, n, h), p, h, kind)
+
+    def local(self):
+        return pltpu.make_async_copy(self.src, self.out.at[:, self.z, self.c, self.n], self.sems[2])
+
+    def drain(self):
+        send = self.sems[1]
+        for kind in range(3):
+            r = self.out.at[:, self.z, self.c, self.n]
+            pltpu.make_async_copy(r, r, send.at[kind]).wait()
+        for kind in range(3, 10):
+            r = self.out.at[:, :, self.c, self.n]
+            pltpu.make_async_copy(r, r, send.at[kind]).wait()
+
+
+def greet():
+    z, c, y, x = place()
+    n = 2 * y + x
+    bar = pltpu.get_barrier_semaphore()
+    who = [(2 * lax.rem(z + k, 4) + c, n) for k in (1, 2, 3)]
+    who += [(2 * z + 1 - c, n), (2 * z + c, 2 * (1 - y) + x), (2 * z + c, 2 * y + 1 - x)]
+    for d in who:
+        pl.semaphore_signal(bar, inc=1, device_id=d, device_id_type=MESH)
+    pl.semaphore_wait(bar, 6)
+
+
+def steps(order, extra=()):
+    seq = [(g, p) for g, a, b in order for p in range(a, b)]
+    n = len(seq)
+    ahead = 3
+    for t in range(n + 3):
+        if t < len(extra):
+            extra[t]()
+        if t == 0:
+            for i in range(min(ahead, n)):
+                seq[i][0].s0(seq[i][1])
+        if t + ahead < n:
+            seq[t + ahead][0].s0(seq[t + ahead][1])
+        if t < n:
+            seq[t][0].s1(seq[t][1])
+        if 0 <= t - 1 < n:
+            seq[t - 1][0].s2(seq[t - 1][1])
+        if 0 <= t - 2 < n:
+            seq[t - 2][0].s3(seq[t - 2][1])
+        if 0 <= t - 3 < n:
+            seq[t - 3][0].s4(seq[t - 3][1])
+
+
+class Total:
+    def __init__(self, acc, came, send, recv):
+        self.acc, self.came, self.send, self.recv = acc, came, send, recv
+        z, c, y, x = place()
+        n = 2 * y + x
+        far = lax.rem(z + 2, 4)
+        near = z + 1 - 2 * lax.rem(z, 2)
+        self.to = [
+            (2 * z + 1 - c, n),
+            (2 * z + c, 2 * y + 1 - x),
+            (2 * z + c, 2 * (1 - y) + x),
+            (2 * near + c, n),
+            (2 * far + c, n),
+        ]
+
+    def copy(self, i):
+        return pltpu.make_async_remote_copy(
+            src_ref=self.acc.at[i], dst_ref=self.came.at[i], send_sem=self.send.at[i],
+            recv_sem=self.recv.at[i], device_id=self.to[i], device_id_type=MESH,
+        )
+
+    def begin(self):
+        self.copy(0).start()
+
+    def step(self, i):
+        self.copy(i).wait_recv()
+        self.acc[i + 1] = self.acc[i] + self.came[i]
+        if i < 4:
+            self.copy(i + 1).start()
+
+    def finish(self):
+        for i in range(5):
+            self.copy(i).wait_send()
+
+
+def gather_kernel(table, a_s, d_s, a_t, d_t, total, A_s, D_s, A_t, D_t, acc, came, ts, tr, *sems):
+    loc = sems[-1]
+    gs = [
+        Gather(src, out, (sems[2 * i], sems[2 * i + 1], loc.at[i]), "cols" if i % 2 == 0 else "rows")
+        for i, (src, out) in enumerate(((a_s, A_s), (d_s, D_s), (a_t, A_t), (d_t, D_t)))
+    ]
+    for g in gs:
+        g.local().start()
+    acc[0] = table[...]
+    greet()
+    tot = Total(acc, came, ts, tr)
+    tot.begin()
+    for g in gs:
+        g.local().wait()
+    steps(
+        [(gs[0], 0, 8), (gs[1], 0, 3), (gs[2], 0, 8), (gs[3], 0, 3)],
+        [functools.partial(tot.step, i) for i in range(5)],
+    )
+    total[...] = acc[5]
+    tot.finish()
+    for g in gs:
+        g.drain()
+
+
+def gather(table, a_s, d_s, a_t, d_t):
+    big = jax.ShapeDtypeStruct((8, 4, 2, 4, 3, 8, 768), BF)
+    down = jax.ShapeDtypeStruct((3, 4, 2, 4, 12, 8, 256), BF)
+    anywhere, vmem = pl.BlockSpec(memory_space=pl.ANY), pl.BlockSpec(memory_space=pltpu.VMEM)
+    dma = pltpu.SemaphoreType.DMA
+    return pl.pallas_call(
+        gather_kernel,
+        out_shape=(jax.ShapeDtypeStruct(table.shape, F32), big, down, big, down),
+        in_specs=[vmem] + [anywhere] * 4,
+        out_specs=(vmem,) * 5,
+        scratch_shapes=[
+            pltpu.VMEM((6, *table.shape), F32),
+            pltpu.VMEM((5, *table.shape), F32),
+            dma((5,)),
+            dma((5,)),
+            dma((8, 2, 10)),
+            dma((10,)),
+            dma((3, 2, 10)),
+            dma((10,)),
+            dma((8, 2, 10)),
+            dma((10,)),
+            dma((3, 2, 10)),
+            dma((10,)),
+            dma((4,)),
+        ],
+        name="gather_weights",
+        compiler_params=pltpu.CompilerParams(
+            collective_id=1, has_side_effects=True, vmem_limit_bytes=56 * 2**20
+        ),
+    )(table, a_s, d_s, a_t, d_t)
+
+
+def pack(w_mix, w_out, w_up, w_down):
+    a = jnp.concatenate([w_mix, w_out, w_up], axis=1)
+    a = a.reshape(3, 8, 8, 768).transpose(2, 0, 1, 3)
+    d = w_down.reshape(12, 8, 3, 256).transpose(2, 0, 1, 3)
+    return a, d
+
+
+def unpack(a, d):
+    a = a.reshape(8, 768, 768)
+    wide = [jnp.concatenate([a[p] for p in group], axis=1) for group in ((0, 1, 2), (3,), (4, 5, 6, 7))]
+    d = d.reshape(3, 3072, 256)
+    return (*wide, jnp.concatenate([d[0], d[1], d[2]], axis=1))
 
 
 def per_device(
@@ -288,21 +535,27 @@
     time_mixer = (time_in, time_out)
     space_shards = (spacemixing, spaceoutput, spaceexpand, spacereduce)
     time_shards = (timemixing, timeoutput, timeexpand, timereduce)
-    tables = lax.psum(
-        jnp.concatenate(
-            [
-                partial_table(cond, spacemodulation, spaceoffsets, here),
-                partial_table(cond, timemodulation, timeoffsets, here),
-            ],
-            axis=0,
-        ),
-        ("wide", "narrow"),
+    partial = jnp.concatenate(
+        [
+            partial_table(cond, spacemodulation, spaceoffsets, here),
+            partial_table(cond, timemodulation, timeoffsets, here),
+        ],
+        axis=0,
     )
     clips = clip_lengths.shape[0]
+    ours = (
+        (lax.axis_size("wide"), lax.axis_size("narrow")) == (8, 4)
+        and spacemixing.shape == (24, 2304)
+        and spacereduce.shape == (96, 768)
+    )
+    if ours:
+        tables, *full = gather(partial, *pack(*space_shards), *pack(*time_shards))
+        space_full, time_full = unpack(*full[:2]), unpack(*full[2:])
+    else:
+        tables = lax.psum(partial, ("wide", "narrow"))
+        space_full, time_full = fetch(space_shards), fetch(time_shards)
     space_table, time_table = tables[:clips], tables[clips:]
     start = tokens.astype(jnp.float32).reshape(frames_own, patches, width)
-    space_full = fetch(space_shards)
-    time_full = fetch(time_shards)
     first, space_kept = forward(start, space_full, space_table, onehot_own, space_mixer)
     second, time_kept = forward(first, time_full, time_table, onehot_own, time_mixer)
     upstream = cotangent.astype(jnp.float32).reshape(frames_own, patches, width)

time: 974 us -> 781 us (0.80)
  waiting for transfers between devices: 600 us -> 258 us
  Pallas kernels: 0 us -> 150 us
  matrix products: 109 us -> 88.5 us
  blocking collectives: 44.6 us -> 61.9 us
    all_gather x2 -> x0, waiting for transfers between devices: 176 us -> none  [fetch(): full = lax.all_gather(packed, ('wide', 'narrow'), axis=0, tiled=True)]
    pallas_call x0 -> x1, Pallas kernels: none -> 150 us  [gather(): pl.pallas_call(gather_kernel, out_shape=(jax.ShapeDtypeStruct(table.shape...]
    psum x1 -> x0, waiting for transfers between devices: 118 us -> none  [per_device(): lax.psum(jnp.concatenate([partial_table(cond, spacemodulation, spaceoffse...]
    all_to_all x1, waiting for transfers between devices: 29 us -> 3.3 us  [time_out(): lax.all_to_all(grads, ('wide', 'narrow'), split_axis=0, concat_axis=1, ti...]
    reduce_scatter x2, waiting for transfers between devices: 234 us -> 213 us  [scatter(): lax.psum_scatter(packed, ('wide', 'narrow'), scatter_dimension=0, tiled=T...]
    all_to_all x0 -> x1, blocking collectives: none -> 17.2 us  [time_in(): lax.all_to_all(result, ('wide', 'narrow'), split_axis=0, concat_axis=1, t...]
    reshape x4 -> x6, local copies, waits for them, and re-layouts: 19.5 us -> 4.83 us  [the longest x4 3.3 us: pack(): d = w_down.reshape(12, 8, 3, 256).transpose(2, 0, 1, 3)]
    unnamed x7 -> x5, other arithmetic: 14.7 us -> 24.4 us
  transfers between devices with their start and end apart: 9 -> 5, of which waited for: 9 -> 5; matrix products, arithmetic and copies ran while one was open for 11% -> 12% of each run, Pallas kernels for 0% -> 0%
where the time goes in v2:
time: 781 us; the launch traced here: 770 us
  waiting for transfers between devices  258 us (33%)
  Pallas kernels  150 us (19%)
  local copies, waits for them, and re-layouts  119 us (15%)
  matrix products  88.5 us (11%)
  other arithmetic  65 us (8%)
  blocking collectives  61.9 us (8%)
  between operations  15.9 us (2%)
  starting transfers between devices  10.8 us (1%)
    reduce_scatter x2, waiting for transfers between devices, scatter(): lax.psum_scatter(packed, ('wide', 'narrow'), scatter_dimension=0, tiled=T...  213 us
    pallas_call x1, Pallas kernels, gather(): pl.pallas_call(gather_kernel, out_shape=(jax.ShapeDtypeStruct(table.shape...  150 us
    psum x1, blocking collectives, per_device(): lax.psum(jnp.concatenate([space_frames, time_frames], axis=0), ('wide', '...  44.6 us
    unnamed x203, local copies, waits for them, and re-layouts  31 us
    dot_general x8, matrix products, outer(): jnp.einsum('fpa,fpb->ab', left, right, preferred_element_type=jnp.float32)  30.2 us
    all_to_all x1, waiting for transfers between devices, time_in(): lax.all_to_all(mixing, ('wide', 'narrow'), split_axis=1, concat_axis=0, t...  28.7 us
    unnamed x5, other arithmetic  24.4 us
    concatenate x2, other arithmetic, scatter(): jnp.concatenate([g.astype(jnp.bfloat16).reshape(rows, -1) for g in grads]...  19.7 us
  transfers between devices with their start and end apart: 5, of which 5 were waited for; matrix products, arithmetic and copies ran while one was open for 12% of the time, Pallas kernels for 0%

profile of v2, /device:TPU:0, one launch (start us, length us, event | category | flops | bytes accessed | tf_op | source)
XLA Modules:
  0.0 769.9 jit_solution(17015985881607747954)
XLA Ops:
  17.7 150.0 %gather_weights.1 = (f32[8,4608]{1,0:T(8,128)}, bf16[8,4,2,4,3,8,768]{6,5,4,3,2,1,0:T(8,128)(2,1)}, bf16[3,4,2,4,12,8,256]{6,5,4,3,2,1,0:T(8,128)(2,1)}, bf16[8,...) custom-call(f32[8,4608]{1,0:T(8,128)} %pad_maximum_fusion.28.table, ...), custom_call_target="tpu_custom_call" | custom-call | tf_op jit(solution)/shard_map/gather_weights/pallas_call | solution.py:428
  172.0 12.2 %fusion.123 = (bf16[1,4,2,4,3,8,768]{6,5,4,3,2,1,0:T(8,128)(2,1)}, bf16[1,4,2,4,3,8,768]{6,5,4,3,2,1,0:T(8,128)(2,1)}, bf16[1,4,2,4,3,8,768]{6,5,4,3,2,1,0:T(8,1...) fusion(bf16[8,4,2,4,3,8,768]{6,5,4,3,2,1,0:T(8,128)(2,1)} %get-, ...), kind=kLoop, calls=%fused_computation.276 | loop fusion | bytes 37748736 | tf_op jit(solution)/shard_map/slice | solution.py:464
  195.0 2.7 fusion.125
  201.5 2.9 fusion.121
  206.4 3.2 copy.167
  210.1 19.7 %reduce.94 = bf16[256,2304]{1,0:T(8,128)(2,1)} reduce(bf16[256,1,2304]{2,1,0:T(2,128)(2,1)} %bitcast.190, bf16[]{:T(256)} %broadcast.502), dimensions={1}, to_apply=%bitcast.182.reduce_sub_computation | reduce | bytes 2359298
  229.9 3.9 reshape.945
  233.8 3.7 all-to-all-start
  237.8 28.7 %all-to-all-done = bf16[32,2,9216]{2,1,0:T(2,128)(2,1)} async-done(((bf16[32,2,9216]{2,1,0:T(2,128)(2,1)}), bf16[32,2,9216]{2,1,0:T(2,128)(2,1)}, u32[]{:S(2)}, u32[]{:S(2)}) %all-to-all-start) | async-done | bytes 1179680 | tf_op jit(solution)/shard_map/all_to_all | solution.py:520
  266.5 5.8 reshape.946
  272.3 9.5 %bitcast_reduce_fusion = bf16[256,2304]{1,0:T(8,128)(2,1)} fusion(bf16[256,1,2304]{2,1,0:T(2,128)(2,1)} %reshape.946), kind=kLoop, calls=%fused_computation.283 | loop fusion | bytes 2359296 | tf_op jit(solution)/shard_map/all_to_all | solution.py:520
  281.9 4.7 reshape.894
  286.6 2.7 fusion.127
  293.3 2.7 reshape.895
  296.0 17.2 %all_to_all.16 = bf16[32,8,768]{2,1,0:T(8,128)(2,1)S(1)} all-to-all(bf16[32,8,768]{2,1,0:T(8,128)(2,1)} %reshape.895), channel_id=1, replica_groups=mesh['wide'=8,'narrow'=4] {'wide','narrow'}, dimensions={0} | all-to-all | bytes 786432 | tf_op jit(solution)/shard_map/all_to_all | solution.py:523
  314.0 2.9 fusion.120
  320.3 3.2 fusion.14
  328.5 4.7 reduce.95
  335.1 3.7 all-to-all-start.2
  338.8 13.6 %all-to-all-done.2 = bf16[32,2,3072]{2,1,0:T(2,128)(2,1)} async-done(((bf16[32,2,3072]{2,1,0:T(2,128)(2,1)}), bf16[32,2,3072]{2,1,0:T(2,128)(2,1)}, u32[]{:S(2)}, u32[]{:S(2)}) %all-to-all-start.2) | async-done | bytes 393248 | tf_op jit(solution)/shard_map/all_to_all | solution.py:528
  352.4 3.4 reshape.948
  355.8 4.2 bitcast_reduce_fusion.1
  360.0 2.4 reshape.897
  362.4 3.5 multiply_reduce_fusion.1
  369.3 2.7 copy.114
  372.0 4.7 convert_element_type.231
  376.8 3.4 all-to-all-start.3
  380.2 3.0 convolution_convert_fusion.8
  383.2 2.5 copy.120
  385.7 6.4 convolution_convert_fusion
  392.1 8.5 %reshape.911 = bf16[768,3072]{1,0:T(8,128)(2,1)} reshape(bf16[3072,768]{1,0:T(8,128)(2,1)} %convolution_convert_fusion) | data formatting | bytes 9437184 | tf_op jit(solution)/shard_map/reshape | solution.py:216
  400.5 5.4 convolution_convert_fusion.1
  405.9 3.3 all-to-all-done.3
  409.2 2.9 convolution_convert_fusion.2
  412.5 10.0 %pad_maximum_fusion.1 = bf16[768,9216]{1,0:T(8,128)(2,1)} fusion(bf16[768,3072]{1,0:T(8,128)(2,1)} %reshape.911, bf16[768,3072]{1,0:T(8,128)(2,1)S(1)} %copy-done.2, bf16[768,768]{1,0:T(8,128)(2,1)S(1)} %copy-done.25, bf16[768,2304]{1,0:T(8,128)(2,1)S(1)} %convolution_convert_fusion.2), kind=kLoop, calls=%fused_computation.1 | loop fusion | flops 56623104 | bytes 28311552 | tf_op jit(solution)/shard_map/concatenate | solution.py:216
  422.7 3.9 multiply_reduce_fusion.4
  429.2 3.0 fusion.63
  433.6 3.4 fusion.7
  443.4 3.0 convolution_convert_fusion.9
  446.4 2.4 copy.119
  448.8 6.7 convolution_convert_fusion.3
  455.5 8.7 %reshape.910 = bf16[768,3072]{1,0:T(8,128)(2,1)} reshape(bf16[3072,768]{1,0:T(8,128)(2,1)} %convolution_convert_fusion.3) | data formatting | bytes 9437184 | tf_op jit(solution)/shard_map/reshape | solution.py:216
  464.2 2.0 multiply_reduce_fusion
  473.1 9.6 %pad_maximum_fusion = bf16[768,9216]{1,0:T(8,128)(2,1)} fusion(bf16[768,3072]{1,0:T(8,128)(2,1)S(1)} %bitcast.185, bf16[768,3072]{1,0:T(8,128)(2,1)S(1)} %convolution_convert_fusion.4, bf16[768,768]{1,0:T(8,128)(2,1)S(1)} %copy-done.24, bf16[768,2304]{1,0:T(8,128)(2,1)S(1)} %convolution_convert_fusion.5), kind=kLoop, calls=%fused_computation | loop fusion | flops 56623104 | bytes 28311552 | tf_op jit(solution)/shard_map/concatenate | solution.py:216
  483.8 3.3 fusion.61
  487.8 44.6 %all-reduce.1 = bf16[8,4608]{1,0:T(8,128)(2,1)S(1)} all-reduce(f32[8,4608]{1,0:T(8,128)S(1)} %pad_maximum_fusion.29), channel_id=1, replica_groups=mesh['wide'=8,'narrow'=4] {'wide','narrow'}, use_global_device_ids=true, to_apply=%region_36.37 | all-reduce | flops 36864 | bytes 221184 | tf_op jit(solution)/shard_map/psum | solution.py:570
  538.7 47.9 %reduce-scatter.5.cloned.1.call-done = bf16[24,9216]{1,0:T(8,128)(2,1)} async-done(((bf16[768,9216]{1,0:T(8,128)(2,1)}), bf16[24,9216]{1,0:T(8,128)(2,1)}) %reduce-scatter.5.cloned.1.call-update) | async-done | bytes 442384 | tf_op jit(solution)/shard_map/reduce_scatter | solution.py:217
  589.2 164.9 %reduce-scatter.3.cloned.1.call-done = bf16[24,9216]{1,0:T(8,128)(2,1)} async-done(((bf16[768,9216]{1,0:T(8,128)(2,1)}), bf16[24,9216]{1,0:T(8,128)(2,1)}) %reduce-scatter.3.cloned.1.call-update) | async-done | bytes 442384 | tf_op jit(solution)/shard_map/reduce_scatter | solution.py:217
  (315 shorter events, 86.5 us)
Async XLA Ops:
  7.2 8.0 %copy-start = (bf16[24,4608]{1,0:T(8,128)(2,1)S(1)}, bf16[24,4608]{1,0:T(8,128)(2,1)}, u32[]{:S(2)}) copy-start(bf16[24,4608]{1,0:T(8,128)(2,1)} %param.21) | copy-start | bytes 663556
  7.2 6.3 copy-start.74
  7.2 6.3 copy-start.76
  7.2 6.3 copy-start.75
  7.2 7.7 %copy-start.80 = (bf16[144]{0:T(256)(128)(2,1)S(1)}, bf16[144]{0:T(256)(128)(2,1)}, u32[]{:S(2)}) copy-start(bf16[144]{0:T(256)(128)(2,1)} %param.28) | copy-start | bytes 868
  7.2 7.8 %copy-start.81 = (bf16[144]{0:T(256)(128)(2,1)S(1)}, bf16[144]{0:T(256)(128)(2,1)}, u32[]{:S(2)}) copy-start(bf16[144]{0:T(256)(128)(2,1)} %param.22) | copy-start | bytes 868
  7.2 8.8 %copy-start.73 = (bf16[24,4608]{1,0:T(8,128)(2,1)S(1)}, bf16[24,4608]{1,0:T(8,128)(2,1)}, u32[]{:S(2)}) copy-start(bf16[24,4608]{1,0:T(8,128)(2,1)} %param.27) | copy-start | bytes 663556
  11.0 160.3 %copy-start.77 = (s32[32,256]{1,0:T(8,128)S(1)}, s32[32,256]{1,0:T(8,128)}, u32[]{:S(2)}) copy-start(s32[32,256]{1,0:T(8,128)} %param.20) | copy-start | bytes 98308
  11.0 160.3 %copy-start.5 = (bf16[256,768]{1,0:T(8,128)(2,1)S(1)}, bf16[256,768]{1,0:T(8,128)(2,1)}, u32[]{:S(2)}) copy-start(bf16[256,768]{1,0:T(8,128)(2,1)} %param.17) | copy-start | bytes 1179652
  171.7 12.4 %copy-start.78 = (f32[256]{0:T(256)}, f32[256]{0:T(256)S(1)}, u32[]{:S(2)}) copy-start(f32[256]{0:T(256)S(1)} %fusion.60) | copy-start | bytes 3076
  190.4 4.1 slice-start.2
  190.4 4.5 slice-start.4
  190.8 4.0 slice-start.3
  190.8 4.2 slice-start.5
  194.2 7.2 copy-start.11
  195.0 3.7 copy-start.60
  195.0 4.9 copy-start.62
  197.8 3.7 copy-start.35
  197.8 3.7 copy-start.37
  197.8 3.7 copy-start.39
  201.5 3.8 copy-start.64
  201.5 3.8 copy-start.65
  201.5 3.8 copy-start.66
  233.8 32.7 %all-to-all-start = ((bf16[32,2,9216]{2,1,0:T(2,128)(2,1)}), bf16[32,2,9216]{2,1,0:T(2,128)(2,1)}, u32[]{:S(2)}, u32[]{:S(2)}) async-start(bf16[32,2,9216]{2,1,0:T(2,128)(2,1)} %reshape.945), calls=%async_computation | async-start | bytes 2359296 | tf_op jit(solution)/shard_map/all_to_all | solution.py:520
  296.0 21.1 %copy-start.67 = (bf16[1,4,2,4,3,8,768]{6,5,4,3,2,1,0:T(8,128)(2,1)S(1)}, bf16[1,4,2,4,3,8,768]{6,5,4,3,2,1,0:T(8,128)(2,1)}, u32[]{:S(2)}) copy-start(bf16[1,4,2,4,3,8,768]{6,5,4,3,2,1,0:T(8,128)(2,1)} %get-tuple-element.69) | copy-start | bytes 3538948
  296.0 21.1 %copy-start.68 = (bf16[1,4,2,4,3,8,768]{6,5,4,3,2,1,0:T(8,128)(2,1)S(1)}, bf16[1,4,2,4,3,8,768]{6,5,4,3,2,1,0:T(8,128)(2,1)}, u32[]{:S(2)}) copy-start(bf16[1,4,2,4,3,8,768]{6,5,4,3,2,1,0:T(8,128)(2,1)} %get-tuple-element.70) | copy-start | bytes 3538948
  296.0 21.1 %copy-start.69 = (bf16[1,4,2,4,3,8,768]{6,5,4,3,2,1,0:T(8,128)(2,1)S(1)}, bf16[1,4,2,4,3,8,768]{6,5,4,3,2,1,0:T(8,128)(2,1)}, u32[]{:S(2)}) copy-start(bf16[1,4,2,4,3,8,768]{6,5,4,3,2,1,0:T(8,128)(2,1)} %get-tuple-element.71) | copy-start | bytes 3538948
  296.0 21.1 %copy-start.70 = (bf16[1,4,2,4,3,8,768]{6,5,4,3,2,1,0:T(8,128)(2,1)S(1)}, bf16[1,4,2,4,3,8,768]{6,5,4,3,2,1,0:T(8,128)(2,1)}, u32[]{:S(2)}) copy-start(bf16[1,4,2,4,3,8,768]{6,5,4,3,2,1,0:T(8,128)(2,1)} %get-tuple-element.72) | copy-start | bytes 3538948
  316.8 8.3 %copy-start.14 = (f32[256,768]{1,0:T(8,128)}, f32[256,768]{1,0:T(8,128)S(1)}, u32[]{:S(2)}) copy-start(f32[256,768]{1,0:T(8,128)S(1)} %get-tuple-element.64) | copy-start | bytes 2359300
  335.1 17.3 %all-to-all-start.2 = ((bf16[32,2,3072]{2,1,0:T(2,128)(2,1)}), bf16[32,2,3072]{2,1,0:T(2,128)(2,1)}, u32[]{:S(2)}, u32[]{:S(2)}) async-start(bf16[32,2,3072]{2,1,0:T(2,128)(2,1)} %reshape.947), calls=%async_computation.2 | async-start | bytes 786432 | tf_op jit(solution)/shard_map/all_to_all | solution.py:528
  362.4 3.6 copy-start.23
  376.8 32.5 %all-to-all-start.3 = ((bf16[32,8,2304]{2,1,0:T(8,128)(2,1)}), bf16[32,8,2304]{2,1,0:T(8,128)(2,1)}, u32[]{:S(2)}, u32[]{:S(2)}) async-start(bf16[32,8,2304]{2,1,0:T(8,128)(2,1)} %convert_element_type.231), calls=%async_computation.3 | async-start | bytes 2359296 | tf_op jit(solution)/shard_map/all_to_all | solution.py:532
  380.1 206.5 %reduce-scatter.5.cloned.1.call-start = ((), (), s32[]{:S(2)}) async-start(), calls=%async_computation.7 | async-start | bytes 14598144 | tf_op jit(solution)/shard_map/reduce_scatter | solution.py:217
  422.6 331.5 %reduce-scatter.3.cloned.1.call-start = ((), (), s32[]{:S(2)}) async-start(), calls=%async_computation.6 | async-start | bytes 14598144 | tf_op jit(solution)/shard_map/reduce_scatter | solution.py:217
  422.6 4.1 copy-start.10
  422.6 4.4 copy-start.15
  422.6 4.4 copy-start.22
  422.7 4.4 copy-start.42
  422.7 4.4 copy-start.44
  422.7 4.9 copy-start.46
  422.7 5.0 copy-start.48
  422.7 5.2 copy-start.71
  422.7 6.3 copy-start.85
  422.7 6.5 copy-start.86
  429.2 4.4 copy-start.83
  432.2 6.9 copy-start.72
  487.1 50.4 %copy-start.17 = (f32[256,768]{1,0:T(8,128)S(1)}, f32[256,768]{1,0:T(8,128)}, u32[]{:S(2)}) copy-start(f32[256,768]{1,0:T(8,128)} %copy-done.16) | copy-start | bytes 2359300
  535.7 226.9 %copy-start.1 = (bf16[24,4608]{1,0:T(8,128)(2,1)S(1)}, bf16[24,4608]{1,0:T(8,128)(2,1)}, u32[]{:S(2)}) copy-start(bf16[24,4608]{1,0:T(8,128)(2,1)} %param.21) | copy-start | bytes 663556
  (50 other events, 111.2 us)
Sparse Core Ops, SparseCore 0:
  422.7 163.9 reduce-scatter.4
  592.6 161.3 reduce-scatter.2

commit v3 on v2

--- a/solution.py
+++ b/solution.py
@@ -120,9 +120,8 @@
     return stacked.reshape(mixing.shape).astype(jnp.bfloat16)
 
 
-def forward(inputs, weights, table, onehot_own, mixer):
+def forward(inputs, weights, mods, mixer):
     w_mix, w_out, w_up, w_down = weights
-    mods = jnp.dot(onehot_own, table, precision=lax.Precision.HIGHEST)[:, None, :]
     pieces = jnp.split(mods, 6, axis=2)
     normed = modulate(inputs, pieces[1], pieces[0]).astype(jnp.bfloat16)
     mixing = jnp.dot(normed, w_mix, preferred_element_type=jnp.float32).astype(jnp.bfloat16)
@@ -328,37 +327,20 @@
             pltpu.make_async_copy(r, r, send.at[kind]).wait()
 
 
+def everyone(me, step):
+    other = lax.rem(me + step, 32)
+    return (other // 4, lax.rem(other, 4))
+
+
 def greet():
-    z, c, y, x = place()
-    n = 2 * y + x
-    bar = pltpu.get_barrier_semaphore()
-    who = [(2 * lax.rem(z + k, 4) + c, n) for k in (1, 2, 3)]
-    who += [(2 * z + 1 - c, n), (2 * z + c, 2 * (1 - y) + x), (2 * z + c, 2 * y + 1 - x)]
-    for d in who:
-        pl.semaphore_signal(bar, inc=1, device_id=d, device_id_type=MESH)
-    pl.semaphore_wait(bar, 6)
-
-
-def steps(order, extra=()):
-    seq = [(g, p) for g, a, b in order for p in range(a, b)]
-    n = len(seq)
-    ahead = 3
-    for t in range(n + 3):
-        if t < len(extra):
-            extra[t]()
-        if t == 0:
-            for i in range(min(ahead, n)):
-                seq[i][0].s0(seq[i][1])
-        if t + ahead < n:
-            seq[t + ahead][0].s0(seq[t + ahead][1])
-        if t < n:
-            seq[t][0].s1(seq[t][1])
-        if 0 <= t - 1 < n:
-            seq[t - 1][0].s2(seq[t - 1][1])
-        if 0 <= t - 2 < n:
-            seq[t - 2][0].s3(seq[t - 2][1])
-        if 0 <= t - 3 < n:
-            seq[t - 3][0].s4(seq[t - 3][1])
+    me = 4 * lax.axis_index("wide") + lax.axis_index("narrow")
+    barrier = pltpu.get_barrier_semaphore()
+
+    @pl.loop(1, 32)
+    def _(i):
+        pl.semaphore_signal(barrier, inc=1, device_id=everyone(me, i), device_id_type=MESH)
+
+    pl.semaphore_wait(barrier, 31)
 
 
 class Total:
@@ -396,60 +378,271 @@
             self.copy(i).wait_send()
 
 
-def gather_kernel(table, a_s, d_s, a_t, d_t, total, A_s, D_s, A_t, D_t, acc, came, ts, tr, *sems):
-    loc = sems[-1]
+def dot(a, b):
+    return jnp.dot(a, b, preferred_element_type=F32)
+
+
+def dot_nt(a, b):
+    return lax.dot_general(a, b, (((1,), (1,)), ((), ())), preferred_element_type=F32)
+
+
+def dot_tn(a, b):
+    return lax.dot_general(a, b, (((0,), (0,)), ((), ())), preferred_element_type=F32)
+
+
+class Mods:
+    def __init__(self, ref, row):
+        self.ref, self.row = ref, row
+
+    def __getitem__(self, k):
+        return self.ref[self.row : self.row + 1, 768 * k : 768 * k + 768]
+
+
+def unit(value):
+    centred = value - jnp.mean(value, axis=-1, keepdims=True)
+    scale = lax.rsqrt(jnp.mean(centred * centred, axis=-1, keepdims=True) + 1e-06)
+    return centred * scale, scale
+
+
+def norm_into(x, mods, shift, scale, out):
+    gain, offset = 1.0 + mods[scale], mods[shift]
+
+    @pl.loop(0, 8)
+    def _(i):
+        rows = pl.ds(32 * i, 32)
+        out[rows, :] = (unit(x[rows, :].astype(F32))[0] * gain + offset).astype(BF)
+
+
+def mix_into(normed, weight, j, mix):
+    @pl.loop(0, 3)
+    def _(t):
+        cols = pl.multiple_of(256 * t, 256)
+        mix[:, pl.ds(768 * j + cols, 256)] = dot(normed[...], weight[j, :, pl.ds(cols, 256)]).astype(BF)
+
+
+def softmax(queries, keys, bias):
+    scores = dot_nt(queries, keys) + bias
+    expo = jnp.exp(scores - jnp.max(scores, axis=-1, keepdims=True))
+    return expo / jnp.sum(expo, axis=-1, keepdims=True)
+
+
+def head_lanes(value, e):
+    lane = lax.broadcasted_iota(jnp.int32, value.shape, 1)
+    return jnp.where((lane < 64) if e == 0 else (lane >= 64), value, jnp.zeros_like(value))
+
+
+def attend(mix, bias, att, first, last):
+    @pl.loop(2 * first, 2 * last)
+    def _(i):
+        j = i // 2
+        rows = pl.ds(pl.multiple_of(128 * lax.rem(i, 2), 128), 128)
+        at = [pl.ds(pl.multiple_of(128 * j + 768 * k, 128), 128) for k in range(3)]
+        queries = mix[rows, at[0]] * jnp.asarray(0.125, BF)
+        keys, values = mix[:, at[1]], mix[:, at[2]]
+        both = [
+            dot(softmax(head_lanes(queries, e), keys, bias[rows, :]).astype(BF), values)
+            for e in range(2)
+        ]
+        lane = lax.broadcasted_iota(jnp.int32, both[0].shape, 1)
+        att[rows, at[0]] = jnp.where(lane < 64, both[0], both[1]).astype(BF)
+
+
+def middle_into(x, att, weight, mods, middle):
+    @pl.loop(0, 3)
+    def _(t):
+        cols = pl.ds(pl.multiple_of(256 * t, 256), 256)
+        gate = mods.ref[mods.row : mods.row + 1, pl.ds(pl.multiple_of(1536 + 256 * t, 256), 256)]
+        middle[:, cols] = x[:, cols].astype(F32) + gate * dot(att[...], weight[3, :, cols])
+
+
+def gelu(h):
+    return 0.5 * h * (1.0 + jnp.tanh(0.7978845608028654 * (h + 0.044715 * (h * h * h))))
+
+
+def active_into(normed, weight, u, active):
+    @pl.loop(0, 6)
+    def _(t):
+        i = lax.rem(t, 3)
+        rows = pl.ds(pl.multiple_of(128 * (t // 3), 128), 128)
+        cols = pl.multiple_of(256 * i, 256)
+        hidden = dot(normed[rows, :], weight[4 + u, :, pl.ds(cols, 256)])
+        active[rows, pl.ds(768 * u + cols, 256)] = gelu(hidden).astype(BF)
+
+
+def result_into(active, down, d, middle, mods, out):
+    cols = slice(256 * d, 256 * d + 256)
+    gate = mods.ref[mods.row : mods.row + 1, 3840 + 256 * d : 4096 + 256 * d]
+
+    @pl.loop(0, 2)
+    def _(i):
+        rows = pl.ds(pl.multiple_of(128 * i, 128), 128)
+        out[rows, cols] = middle[rows, cols] + gate * dot(active[rows, :], down[d])
+
+
+class Spread:
+    def __init__(self, src, dst, sems):
+        self.src, self.dst = src, dst
+        self.send, self.recv, self.local = sems
+
+    def start(self):
+        me = 4 * lax.axis_index("wide") + lax.axis_index("narrow")
+        pltpu.make_async_copy(self.src.at[me], self.dst.at[me], self.local).start()
+
+        @pl.loop(1, 32)
+        def _(i):
+            to = everyone(me, i)
+            pltpu.make_async_remote_copy(
+                src_ref=self.src.at[4 * to[0] + to[1]], dst_ref=self.dst.at[me], send_sem=self.send,
+                recv_sem=self.recv, device_id=to, device_id_type=MESH,
+            ).start()
+
+    def wait(self):
+        one, most = self.dst.at[0], self.dst.at[pl.ds(0, 31)]
+        pltpu.make_async_copy(one, one, self.local).wait()
+        pltpu.make_async_copy(most, most, self.send).wait()
+        pltpu.make_async_copy(most, most, self.recv).wait()
+
+
+def forward_kernel(
+    tokens, table, pick, space_bias, time_bias, a_s, d_s, a_t, d_t,
+    first, second, mods, mix_s, att_s, mix_t, att_t, A_s, D_s, A_t, D_t,
+    acc, came, normed, middle, active, mix_own, att_own, wa_s, wd_s, wa_t, wd_t, ts, tr, hop, *sems,
+):
+    loc, back = sems[-2], sems[-1]
     gs = [
         Gather(src, out, (sems[2 * i], sems[2 * i + 1], loc.at[i]), "cols" if i % 2 == 0 else "rows")
-        for i, (src, out) in enumerate(((a_s, A_s), (d_s, D_s), (a_t, A_t), (d_t, D_t)))
+        for i, (src, out) in enumerate(((a_s, wa_s), (d_s, wd_s), (a_t, wa_t), (d_t, wd_t)))
     ]
+    outs = (A_s, D_s, A_t, D_t)
     for g in gs:
         g.local().start()
     acc[0] = table[...]
     greet()
-    tot = Total(acc, came, ts, tr)
-    tot.begin()
-    for g in gs:
-        g.local().wait()
-    steps(
-        [(gs[0], 0, 8), (gs[1], 0, 3), (gs[2], 0, 8), (gs[3], 0, 3)],
-        [functools.partial(tot.step, i) for i in range(5)],
-    )
-    total[...] = acc[5]
-    tot.finish()
+    total = Total(acc, came, ts, tr)
+    total.begin()
+    seq = [(i, p) for i, count in enumerate((8, 3, 8, 3)) for p in range(count)]
+    stored = []
+    done = [0]
+
+    def tick():
+        t = done[0]
+        done[0] += 1
+        if t == 0:
+            for i, p in seq[:3]:
+                gs[i].s0(p)
+            for g in gs:
+                g.local().wait()
+        if t + 3 < len(seq):
+            i, p = seq[t + 3]
+            gs[i].s0(p)
+        for lag, stage in enumerate(("s1", "s2", "s3", "s4")):
+            if 0 <= t - lag < len(seq):
+                i, p = seq[t - lag]
+                getattr(gs[i], stage)(p)
+                if lag == 3:
+                    copy = pltpu.make_async_copy(gs[i].out.at[p], outs[i].at[p], back.at[t - lag])
+                    copy.start()
+                    stored.append(copy)
+        if 1 <= t <= 5:
+            total.step(t - 1)
+
+    def need(i):
+        while done[0] < min(i + 4, len(seq) + 3):
+            tick()
+
+    def run(base, x, row, mixer, att, weight, down, out):
+        vec = Mods(mods, row)
+        mix = mixer[0]
+        need(base)
+        norm_into(x, vec, 0, 1, normed)
+        for j in range(3):
+            need(base + j)
+            mix_into(normed, weight, j, mix)
+        mixer[1]()
+        need(base + 3)
+        middle_into(x, att, weight, vec, middle)
+        norm_into(middle, vec, 3, 4, normed)
+        for u in range(4):
+            need(base + 4 + u)
+            active_into(normed, weight, u, active)
+        for d in range(3):
+            need(base + 8 + d)
+            result_into(active, down, d, middle, vec, out)
+
+    while done[0] < 6:
+        tick()
+    mods[...] = jnp.zeros_like(mods)
+    for row in range(2):
+        mods[row : row + 1, :] = jnp.sum(acc[5] * pick[:, row : row + 1], axis=0, keepdims=True)
+    total.finish()
+
+    def flat(ref):
+        return ref.reshape(256, ref.shape[-1])
+
+    def views(a, d):
+        return a.reshape(8, 768, 768), d.reshape(3, 3072, 256)
+
+    def space_mixer():
+        attend(flat(mix_s), space_bias, flat(att_s), 0, 3)
+        tick()
+        attend(flat(mix_s), space_bias, flat(att_s), 3, 6)
+
+    def time_mixer():
+        out = Spread(mix_own, mix_t, (hop.at[0], hop.at[1], hop.at[2]))
+        out.start()
+        need(15)
+        out.wait()
+        attend(flat(mix_t), time_bias, flat(att_own), 0, 6)
+        home = Spread(att_own, att_t, (hop.at[3], hop.at[4], hop.at[5]))
+        home.start()
+        need(16)
+        home.wait()
+
+    run(0, tokens, 0, (flat(mix_s), space_mixer), flat(att_s), *views(wa_s, wd_s), first)
+    run(11, first, 1, (flat(mix_own), time_mixer), flat(att_t), *views(wa_t, wd_t), second)
+    while done[0] < len(seq) + 3:
+        tick()
+    for copy in stored:
+        copy.wait()
     for g in gs:
         g.drain()
 
 
-def gather(table, a_s, d_s, a_t, d_t):
-    big = jax.ShapeDtypeStruct((8, 4, 2, 4, 3, 8, 768), BF)
-    down = jax.ShapeDtypeStruct((3, 4, 2, 4, 12, 8, 256), BF)
+def forward_all(tokens, table, pick, space_bias, time_bias, space_packed, time_packed):
+    shape = jax.ShapeDtypeStruct
+    big, down = shape((8, 4, 2, 4, 3, 8, 768), BF), shape((3, 4, 2, 4, 12, 8, 256), BF)
     anywhere, vmem = pl.BlockSpec(memory_space=pl.ANY), pl.BlockSpec(memory_space=pltpu.VMEM)
-    dma = pltpu.SemaphoreType.DMA
+    dma, mem = pltpu.SemaphoreType.DMA, pltpu.VMEM
+    wide, slim = shape((32, 8, 2304), BF), shape((32, 8, 768), BF)
+    plane = shape((256, 768), F32)
     return pl.pallas_call(
-        gather_kernel,
-        out_shape=(jax.ShapeDtypeStruct(table.shape, F32), big, down, big, down),
-        in_specs=[vmem] + [anywhere] * 4,
-        out_specs=(vmem,) * 5,
+        forward_kernel,
+        out_shape=(
+            plane, plane, shape((8, 4608), F32), wide, slim, wide, slim, big, down, big, down,
+        ),
+        in_specs=[vmem] * 5 + [anywhere] * 4,
+        out_specs=(vmem,) * 7 + (anywhere,) * 4,
         scratch_shapes=[
-            pltpu.VMEM((6, *table.shape), F32),
-            pltpu.VMEM((5, *table.shape), F32),
+            mem((6, *table.shape), F32),
+            mem((5, *table.shape), F32),
+            mem((256, 768), BF),
+            mem((256, 768), F32),
+            mem((256, 3072), BF),
+            mem(wide.shape, BF),
+            mem(slim.shape, BF),
+            *(mem(a.shape, BF) for a in (big, down, big, down)),
             dma((5,)),
             dma((5,)),
-            dma((8, 2, 10)),
-            dma((10,)),
-            dma((3, 2, 10)),
-            dma((10,)),
-            dma((8, 2, 10)),
-            dma((10,)),
-            dma((3, 2, 10)),
-            dma((10,)),
+            dma((6,)),
+            *(dma(s) for s in ((8, 2, 10), (10,), (3, 2, 10), (10,)) * 2),
             dma((4,)),
+            dma((22,)),
         ],
-        name="gather_weights",
+        name="forward_blocks",
         compiler_params=pltpu.CompilerParams(
             collective_id=1, has_side_effects=True, vmem_limit_bytes=56 * 2**20
         ),
-    )(table, a_s, d_s, a_t, d_t)
+    )(tokens, table, pick, space_bias, time_bias, *space_packed, *time_packed)
 
 
 def pack(w_mix, w_out, w_up, w_down):
@@ -548,16 +741,42 @@
         and spacemixing.shape == (24, 2304)
         and spacereduce.shape == (96, 768)
     )
+    start = tokens.astype(jnp.float32).reshape(frames_own, patches, width)
     if ours:
-        tables, *full = gather(partial, *pack(*space_shards), *pack(*time_shards))
-        space_full, time_full = unpack(*full[:2]), unpack(*full[2:])
+        own_clip = onehot_own[0]
+        none = jnp.zeros_like(own_clip)
+        pick = jnp.stack(
+            [jnp.concatenate([own_clip, none]), jnp.concatenate([none, own_clip])], axis=1
+        )
+        space_bias = jnp.where(space_allowed[0], 0.0, -1e30)
+        places = lambda v: jnp.broadcast_to(v, (32, 8)).reshape(256)
+        clip_of, patch_of = places(segment[:, None]), places(jnp.arange(8)[None])
+        keep_of = places(keep_cols)
+        time_bias = jnp.where(
+            (patch_of[:, None] == patch_of[None, :])
+            & (clip_of[:, None] == clip_of[None, :])
+            & (keep_of[None, :] | jnp.eye(256, dtype=bool)),
+            0.0,
+            -1e30,
+        )
+        saved = forward_all(
+            tokens, partial, pick, space_bias, time_bias, pack(*space_shards), pack(*time_shards)
+        )
+        space_full, time_full = unpack(*saved[7:9]), unpack(*saved[9:11])
+        rows = saved[2]
+        space_mods, time_mods = rows[0:1, None, :], rows[1:2, None, :]
     else:
         tables = lax.psum(partial, ("wide", "narrow"))
         space_full, time_full = fetch(space_shards), fetch(time_shards)
-    space_table, time_table = tables[:clips], tables[clips:]
-    start = tokens.astype(jnp.float32).reshape(frames_own, patches, width)
-    first, space_kept = forward(start, space_full, space_table, onehot_own, space_mixer)
-    second, time_kept = forward(first, time_full, time_table, onehot_own, time_mixer)
+        own_table = lambda table: jnp.dot(onehot_own, table, precision=lax.Precision.HIGHEST)
+        space_mods = own_table(tables[:clips])[:, None, :]
+        time_mods = own_table(tables[clips:])[:, None, :]
+    first, space_kept = forward(start, space_full, space_mods, space_mixer)
+    if ours:
+        first = saved[0].reshape(start.shape)
+    second, time_kept = forward(first, time_full, time_mods, time_mixer)
+    if ours:
+        second = saved[1].reshape(start.shape)
     upstream = cotangent.astype(jnp.float32).reshape(frames_own, patches, width)
     grad_first, time_frames, time_raw = backward(
         time_kept, time_full, upstream, onehot_own, time_mixer

time: 781 us -> 782 us (level)
  Pallas kernels: 150 us -> 190 us
  waiting for transfers between devices: 258 us -> 236 us
  blocking collectives: 61.9 us -> 42.6 us
    pallas_call x1, Pallas kernels: 150 us -> 190 us  [forward_all(): pl.pallas_call(forward_kernel, out_shape=(plane, plane, shape((8, 4608),...]
    reduce_scatter x2, waiting for transfers between devices: 213 us -> 180 us  [scatter(): lax.psum_scatter(packed, ('wide', 'narrow'), scatter_dimension=0, tiled=T...]
    all_to_all x1 -> x0, blocking collectives: 17.2 us -> none  [time_in(): lax.all_to_all(result, ('wide', 'narrow'), split_axis=0, concat_axis=1, t...]
    unnamed x5 -> x4, other arithmetic: 24.4 us -> 13.5 us
    all_to_all x0 -> x1, waiting for transfers between devices: none -> 8.99 us  [time_in(): lax.all_to_all(result, ('wide', 'narrow'), split_axis=0, concat_axis=1, t...]
    unnamed x203 -> x285, local copies, waits for them, and re-layouts: 31 us -> 30.4 us
  transfers between devices with their start and end apart: 5 -> 6, of which waited for: 5 -> 6; matrix products, arithmetic and copies ran while one was open for 12% -> 16% of each run, Pallas kernels for 0% -> 0%
where the time goes in v3:
time: 782 us; the launch traced here: 770 us
  waiting for transfers between devices  236 us (30%)
  Pallas kernels  190 us (24%)
  local copies, waits for them, and re-layouts  119 us (15%)
  matrix products  86.3 us (11%)
  other arithmetic  64.9 us (8%)
  blocking collectives  42.6 us (5%)
  between operations  16.5 us (2%)
  starting transfers between devices  15.7 us (2%)
    pallas_call x1, Pallas kernels, forward_all(): pl.pallas_call(forward_kernel, out_shape=(plane, plane, shape((8, 4608),...  190 us
    reduce_scatter x2, waiting for transfers between devices, scatter(): lax.psum_scatter(packed, ('wide', 'narrow'), scatter_dimension=0, tiled=T...  180 us
    psum x1, blocking collectives, per_device(): lax.psum(jnp.concatenate([space_frames, time_frames], axis=0), ('wide', '...  42.6 us
    unnamed x285, local copies, waits for them, and re-layouts  30.4 us
    all_to_all x1, waiting for transfers between devices, time_in(): lax.all_to_all(mixing, ('wide', 'narrow'), split_axis=1, concat_axis=0, t...  28.7 us
    dot_general x8, matrix products, outer(): jnp.einsum('fpa,fpb->ab', left, right, preferred_element_type=jnp.float32)  28.7 us
    dot_general x8, matrix products, against(): lax.dot_general(left, weight, (((left.ndim - 1,), (1,)), ((), ())), prefe...  21.7 us
    concatenate x2, other arithmetic, scatter(): jnp.concatenate([g.astype(jnp.bfloat16).reshape(rows, -1) for g in grads]...  19.2 us
  transfers between devices with their start and end apart: 6, of which 6 were waited for; matrix products, arithmetic and copies ran while one was open for 16% of the time, Pallas kernels for 0%

profile of v3, /device:TPU:0, one launch (start us, length us, event | category | flops | bytes accessed | tf_op | source)
XLA Modules:
  0.0 770.4 jit_solution(8656401107652532125)
XLA Ops:
  20.5 189.9 %forward_blocks.1 = (f32[256,768]{1,0:T(8,128)}, f32[256,768]{1,0:T(8,128)}, f32[8,4608]{1,0:T(8,128)}, bf16[32,8,2304]{2,1,0:T(8,128)(2,1)}, bf16[32,8,768]{2,1...) custom-call(bf16[256,768]{1,0:T(8,128)(2,1)} %tokens.1, ...), custom_call_target="tpu_custom_call" | custom-call | tf_op jit(solution)/shard_map/forward_blocks/pallas_call | solution.py:618
  215.4 6.7 fusion.123
  227.5 8.8 %reduce.94 = bf16[256,2304]{1,0:T(8,128)(2,1)} reduce(bf16[256,1,2304]{2,1,0:T(2,128)(2,1)S(1)} %bitcast.185, bf16[]{:T(256)} %broadcast.493), dimensions={1}, to_apply=%bitcast.177.reduce_sub_computation | reduce | bytes 2359298
  236.3 3.9 reshape.939
  240.2 4.7 all-to-all-start
  245.3 28.7 %all-to-all-done = bf16[32,2,9216]{2,1,0:T(2,128)(2,1)} async-done(((bf16[32,2,9216]{2,1,0:T(2,128)(2,1)}), bf16[32,2,9216]{2,1,0:T(2,128)(2,1)}, u32[]{:S(2)}, u32[]{:S(2)}) %all-to-all-start) | async-done | bytes 1179680 | tf_op jit(solution)/shard_map/all_to_all | solution.py:713
  274.0 4.3 reshape.940
  278.3 7.9 %bitcast_reduce_fusion = bf16[256,2304]{1,0:T(8,128)(2,1)} fusion(bf16[256,1,2304]{2,1,0:T(2,128)(2,1)S(1)} %reshape.940), kind=kLoop, calls=%fused_computation.282 | loop fusion | bytes 2359296 | tf_op jit(solution)/shard_map/all_to_all | solution.py:713
  286.2 4.7 reshape.887
  290.8 2.7 fusion.126
  298.0 3.8 all-to-all-start.1
  301.8 4.6 fusion.125
  306.4 9.0 %all-to-all-done.1 = bf16[32,8,768]{2,1,0:T(8,128)(2,1)S(1)} async-done(((bf16[32,8,768]{2,1,0:T(8,128)(2,1)}), bf16[32,8,768]{2,1,0:T(8,128)(2,1)S(1)}, u32[]{:S(2)}, u32[]{:S(2)}) %all-to-all-start.1) | async-done | bytes 393248 | tf_op jit(solution)/shard_map/all_to_all | solution.py:716
  315.4 2.8 fusion.121
  321.0 3.2 fusion.7
  324.3 2.1 multiply_reduce_fusion.2
  329.7 4.7 reduce.95
  336.3 3.7 all-to-all-start.2
  341.5 12.1 %all-to-all-done.2 = bf16[32,2,3072]{2,1,0:T(2,128)(2,1)} async-done(((bf16[32,2,3072]{2,1,0:T(2,128)(2,1)}), bf16[32,2,3072]{2,1,0:T(2,128)(2,1)}, u32[]{:S(2)}, u32[]{:S(2)}) %all-to-all-start.2) | async-done | bytes 393248 | tf_op jit(solution)/shard_map/all_to_all | solution.py:721
  353.6 3.5 reshape.942
  357.1 4.2 bitcast_reduce_fusion.1
  361.2 2.5 reshape.890
  363.7 3.0 multiply_reduce_fusion.1
  370.1 2.7 copy.121
  372.8 4.9 convert_element_type.224
  377.6 3.4 all-to-all-start.3
  384.5 6.3 convolution_convert_fusion
  390.7 8.5 %reshape.910 = bf16[768,3072]{1,0:T(8,128)(2,1)} reshape(bf16[3072,768]{1,0:T(8,128)(2,1)} %convolution_convert_fusion) | data formatting | bytes 9437184 | tf_op jit(solution)/shard_map/reshape | solution.py:215
  399.3 5.1 convolution_convert_fusion.1
  404.4 5.7 all-to-all-done.3
  410.1 2.7 convolution_convert_fusion.2
  412.8 10.0 %pad_maximum_fusion.1 = bf16[768,9216]{1,0:T(8,128)(2,1)} fusion(bf16[768,3072]{1,0:T(8,128)(2,1)} %reshape.910, bf16[768,3072]{1,0:T(8,128)(2,1)S(1)} %copy-done.5, bf16[768,768]{1,0:T(8,128)(2,1)S(1)} %copy.130, bf16[768,2304]{1,0:T(8,128)(2,1)S(1)} %convolution_convert_fusion.2), kind=kLoop, calls=%fused_computation.1 | loop fusion | flops 56623104 | bytes 28311552 | tf_op jit(solution)/shard_map/concatenate | solution.py:215
  425.4 7.1 fusion.122
  439.2 2.3 fusion.34
  449.4 4.4 multiply_reduce_fusion.4
  455.2 3.1 fusion.14
  462.5 2.5 convolution_convert_fusion.12
  466.9 2.9 convolution_convert_fusion.9
  469.8 2.7 copy.129
  472.5 7.2 convolution_convert_fusion.3
  479.7 8.5 %reshape.909 = bf16[768,3072]{1,0:T(8,128)(2,1)} reshape(bf16[3072,768]{1,0:T(8,128)(2,1)} %convolution_convert_fusion.3) | data formatting | bytes 9437184 | tf_op jit(solution)/shard_map/reshape | solution.py:215
  496.9 9.2 %pad_maximum_fusion = bf16[768,9216]{1,0:T(8,128)(2,1)} fusion(bf16[768,3072]{1,0:T(8,128)(2,1)S(1)} %bitcast.180, bf16[768,3072]{1,0:T(8,128)(2,1)S(1)} %convolution_convert_fusion.4, bf16[768,768]{1,0:T(8,128)(2,1)S(1)} %copy-done.15, bf16[768,2304]{1,0:T(8,128)(2,1)S(1)} %convolution_convert_fusion.5), kind=kLoop, calls=%fused_computation | loop fusion | flops 56623104 | bytes 28311552 | tf_op jit(solution)/shard_map/concatenate | solution.py:215
  507.6 4.9 fusion.48
  512.8 3.7 fusion.66
  519.8 42.6 %all-reduce.3 = bf16[8,4608]{1,0:T(8,128)(2,1)S(1)} all-reduce(f32[8,4608]{1,0:T(8,128)S(1)} %pad_maximum_fusion.37), channel_id=1, replica_groups=mesh['wide'=8,'narrow'=4] {'wide','narrow'}, use_global_device_ids=true, to_apply=%region_36.37 | all-reduce | flops 36864 | bytes 221184 | tf_op jit(solution)/shard_map/psum | solution.py:789
  567.4 2.4 add_add_fusion.4
  569.8 15.4 %reduce-scatter.5.cloned.1.call-done = bf16[24,9216]{1,0:T(8,128)(2,1)} async-done(((bf16[768,9216]{1,0:T(8,128)(2,1)}), bf16[24,9216]{1,0:T(8,128)(2,1)}) %reduce-scatter.5.cloned.1.call-update) | async-done | bytes 442384 | tf_op jit(solution)/shard_map/reduce_scatter | solution.py:216
  587.7 165.0 %reduce-scatter.3.cloned.1.call-done = bf16[24,9216]{1,0:T(8,128)(2,1)} async-done(((bf16[768,9216]{1,0:T(8,128)(2,1)}), bf16[24,9216]{1,0:T(8,128)(2,1)}) %reduce-scatter.3.cloned.1.call-update) | async-done | bytes 442384 | tf_op jit(solution)/shard_map/reduce_scatter | solution.py:216
  (409 shorter events, 99.5 us)
Async XLA Ops:
  7.2 8.2 %copy-start = (bf16[24,4608]{1,0:T(8,128)(2,1)S(1)}, bf16[24,4608]{1,0:T(8,128)(2,1)}, u32[]{:S(2)}) copy-start(bf16[24,4608]{1,0:T(8,128)(2,1)} %param.21) | copy-start | bytes 663556
  7.2 8.0 %copy-start.124 = (bf16[144]{0:T(256)(128)(2,1)S(1)}, bf16[144]{0:T(256)(128)(2,1)}, u32[]{:S(2)}) copy-start(bf16[144]{0:T(256)(128)(2,1)} %param.28) | copy-start | bytes 868
  7.2 8.1 %copy-start.125 = (bf16[144]{0:T(256)(128)(2,1)S(1)}, bf16[144]{0:T(256)(128)(2,1)}, u32[]{:S(2)}) copy-start(bf16[144]{0:T(256)(128)(2,1)} %param.22) | copy-start | bytes 868
  7.2 9.1 %copy-start.65 = (bf16[24,4608]{1,0:T(8,128)(2,1)S(1)}, bf16[24,4608]{1,0:T(8,128)(2,1)}, u32[]{:S(2)}) copy-start(bf16[24,4608]{1,0:T(8,128)(2,1)} %param.27) | copy-start | bytes 663556
  9.1 11.5 %copy-start.112 = (pred[256]{0:T(512)(128)(4,1)}, pred[256]{0:T(512)(128)(4,1)S(1)}, u32[]{:S(2)}) copy-start(pred[256]{0:T(512)(128)(4,1)S(1)} %compare_reduce_fusion) | copy-start | bytes 772
  211.7 10.4 %copy-start.89 = (f32[256]{0:T(256)}, f32[256]{0:T(256)S(1)}, u32[]{:S(2)}) copy-start(f32[256]{0:T(256)S(1)} %broadcast_multiply_fusion.5) | copy-start | bytes 3076
  213.1 9.1 %copy-start.101 = (f32[256]{0:T(256)}, f32[256]{0:T(256)S(1)}, u32[]{:S(2)}) copy-start(f32[256]{0:T(256)S(1)} %fusion.93) | copy-start | bytes 3076
  215.4 194.7 %copy-start.69 = (f32[768]{0:T(1024)}, f32[768]{0:T(1024)S(1)}, u32[]{:S(2)}) copy-start(f32[768]{0:T(1024)S(1)} %get-tuple-element.53) | copy-start | bytes 9220
  215.4 8.6 %copy-start.2 = (f32[256,768]{1,0:T(8,128)S(1)}, f32[256,768]{1,0:T(8,128)}, u32[]{:S(2)}) copy-start(f32[256,768]{1,0:T(8,128)} %get-tuple-element.142) | copy-start | bytes 2359300
  236.3 8.6 %copy-start.85 = (s32[32,256]{1,0:T(8,128)S(1)}, s32[32,256]{1,0:T(8,128)}, u32[]{:S(2)}) copy-start(s32[32,256]{1,0:T(8,128)} %param.20) | copy-start | bytes 98308
  240.2 33.8 %all-to-all-start = ((bf16[32,2,9216]{2,1,0:T(2,128)(2,1)}), bf16[32,2,9216]{2,1,0:T(2,128)(2,1)}, u32[]{:S(2)}, u32[]{:S(2)}) async-start(bf16[32,2,9216]{2,1,0:T(2,128)(2,1)} %reshape.939), calls=%async_computation | async-start | bytes 2359296 | tf_op jit(solution)/shard_map/all_to_all | solution.py:713
  298.0 17.4 %all-to-all-start.1 = ((bf16[32,8,768]{2,1,0:T(8,128)(2,1)}), bf16[32,8,768]{2,1,0:T(8,128)(2,1)S(1)}, u32[]{:S(2)}, u32[]{:S(2)}) async-start(bf16[32,8,768]{2,1,0:T(8,128)(2,1)} %reshape.888), calls=%async_computation.1 | async-start | bytes 786432 | tf_op jit(solution)/shard_map/all_to_all | solution.py:716
  318.2 8.2 %copy-start.94 = (f32[256]{0:T(256)}, f32[256]{0:T(256)S(1)}, u32[]{:S(2)}) copy-start(f32[256]{0:T(256)S(1)} %broadcast_multiply_fusion.4) | copy-start | bytes 3076
  318.5 7.9 %copy-start.106 = (f32[256]{0:T(256)}, f32[256]{0:T(256)S(1)}, u32[]{:S(2)}) copy-start(f32[256]{0:T(256)S(1)} %fusion.94) | copy-start | bytes 3076
  336.3 17.3 %all-to-all-start.2 = ((bf16[32,2,3072]{2,1,0:T(2,128)(2,1)}), bf16[32,2,3072]{2,1,0:T(2,128)(2,1)}, u32[]{:S(2)}, u32[]{:S(2)}) async-start(bf16[32,2,3072]{2,1,0:T(2,128)(2,1)} %reshape.941), calls=%async_computation.2 | async-start | bytes 786432 | tf_op jit(solution)/shard_map/all_to_all | solution.py:721
  372.8 8.3 %copy-start.10 = (f32[256,768]{1,0:T(8,128)S(1)}, f32[256,768]{1,0:T(8,128)}, u32[]{:S(2)}) copy-start(f32[256,768]{1,0:T(8,128)} %copy-done.9) | copy-start | bytes 2359300
  372.8 8.3 %copy-start.18 = (bf16[256,768]{1,0:T(8,128)(2,1)S(1)}, bf16[256,768]{1,0:T(8,128)(2,1)}, u32[]{:S(2)}) copy-start(bf16[256,768]{1,0:T(8,128)(2,1)} %param.33) | copy-start | bytes 1179652
  372.8 8.3 %copy-start.79 = (f32[768]{0:T(1024)S(1)}, f32[768]{0:T(1024)}, u32[]{:S(2)}) copy-start(f32[768]{0:T(1024)} %get-tuple-element.54) | copy-start | bytes 9220
  372.8 8.3 %copy-start.97 = (f32[256]{0:T(256)S(1)}, f32[256]{0:T(256)}, u32[]{:S(2)}) copy-start(f32[256]{0:T(256)} %copy-done.96) | copy-start | bytes 3076
  377.6 32.5 %all-to-all-start.3 = ((bf16[32,8,2304]{2,1,0:T(8,128)(2,1)}), bf16[32,8,2304]{2,1,0:T(8,128)(2,1)}, u32[]{:S(2)}, u32[]{:S(2)}) async-start(bf16[32,8,2304]{2,1,0:T(8,128)(2,1)} %convert_element_type.224), calls=%async_computation.3 | async-start | bytes 2359296 | tf_op jit(solution)/shard_map/all_to_all | solution.py:725
  381.0 204.1 %reduce-scatter.5.cloned.1.call-start = ((), (), s32[]{:S(2)}) async-start(), calls=%async_computation.7 | async-start | bytes 14598144 | tf_op jit(solution)/shard_map/reduce_scatter | solution.py:216
  390.7 8.5 %copy-start.95 = (f32[256]{0:T(256)S(1)}, f32[256]{0:T(256)}, u32[]{:S(2)}) copy-start(f32[256]{0:T(256)} %copy-done.94) | copy-start | bytes 3076
  390.7 8.5 %copy-start.107 = (f32[256]{0:T(256)S(1)}, f32[256]{0:T(256)}, u32[]{:S(2)}) copy-start(f32[256]{0:T(256)} %copy-done.106) | copy-start | bytes 3076
  399.2 10.8 %copy-start.90 = (f32[256]{0:T(256)S(1)}, f32[256]{0:T(256)}, u32[]{:S(2)}) copy-start(f32[256]{0:T(256)} %copy-done.89) | copy-start | bytes 3076
  399.2 10.8 %copy-start.102 = (f32[256]{0:T(256)S(1)}, f32[256]{0:T(256)}, u32[]{:S(2)}) copy-start(f32[256]{0:T(256)} %copy-done.101) | copy-start | bytes 3076
  422.9 329.9 %reduce-scatter.3.cloned.1.call-start = ((), (), s32[]{:S(2)}) async-start(), calls=%async_computation.6 | async-start | bytes 14598144 | tf_op jit(solution)/shard_map/reduce_scatter | solution.py:216
  425.0 7.5 copy-start.66
  425.0 7.6 copy-start.75
  425.0 16.5 %copy-start.80 = (f32[768]{0:T(1024)}, f32[768]{0:T(1024)S(1)}, u32[]{:S(2)}) copy-start(f32[768]{0:T(1024)S(1)} %get-tuple-element.48) | copy-start | bytes 9220
  425.1 7.4 copy-start.82
  425.4 7.1 copy-start.110
  425.4 7.1 copy-start.86
  442.1 18.3 %copy-start.7 = (f32[256,768]{1,0:T(8,128)}, f32[256,768]{1,0:T(8,128)S(1)}, u32[]{:S(2)}) copy-start(f32[256,768]{1,0:T(8,128)S(1)} %get-tuple-element.60) | copy-start | bytes 2359300
  442.1 18.3 %copy-start.92 = (f32[256]{0:T(256)}, f32[256]{0:T(256)S(1)}, u32[]{:S(2)}) copy-start(f32[256]{0:T(256)S(1)} %broadcast_multiply_fusion.2) | copy-start | bytes 3076
  442.4 18.1 %copy-start.104 = (f32[256]{0:T(256)}, f32[256]{0:T(256)S(1)}, u32[]{:S(2)}) copy-start(f32[256]{0:T(256)S(1)} %fusion.96) | copy-start | bytes 3076
  443.0 12.1 %copy-start.34 = (bf16[1,4,2,4,12,8,256]{6,5,4,3,2,1,0:T(8,128)(2,1)}, bf16[1,4,2,4,12,8,256]{6,5,4,3,2,1,0:T(8,128)(2,1)S(1)}, u32[]{:S(2)}) copy-start(bf16[1,4,2,4,12,8,256]{6,5,4,3,2,1,0:T(8,128)(2,1)S(1)} %get-tuple-element.83) | copy-start | bytes 4718596
  443.1 12.1 %copy-start.36 = (bf16[1,4,2,4,12,8,256]{6,5,4,3,2,1,0:T(8,128)(2,1)}, bf16[1,4,2,4,12,8,256]{6,5,4,3,2,1,0:T(8,128)(2,1)S(1)}, u32[]{:S(2)}) copy-start(bf16[1,4,2,4,12,8,256]{6,5,4,3,2,1,0:T(8,128)(2,1)S(1)} %get-tuple-element.84) | copy-start | bytes 4718596
  443.1 12.1 %copy-start.38 = (bf16[1,4,2,4,12,8,256]{6,5,4,3,2,1,0:T(8,128)(2,1)}, bf16[1,4,2,4,12,8,256]{6,5,4,3,2,1,0:T(8,128)(2,1)S(1)}, u32[]{:S(2)}) copy-start(bf16[1,4,2,4,12,8,256]{6,5,4,3,2,1,0:T(8,128)(2,1)S(1)} %get-tuple-element.85) | copy-start | bytes 4718596
  449.4 5.8 copy-start.126
  455.2 5.7 copy-start.28
  507.6 5.0 copy-start.100
  507.6 5.0 copy-start.115
  507.6 5.0 copy-start.114
  507.6 5.1 copy-start.68
  507.6 5.1 copy-start.84
  567.4 194.0 %copy-start.4 = (f32[256,768]{1,0:T(8,128)S(1)}, f32[256,768]{1,0:T(8,128)}, u32[]{:S(2)}) copy-start(f32[256,768]{1,0:T(8,128)} %get-tuple-element.142) | copy-start | bytes 2359300
  569.8 192.5 %copy-start.62 = (f32[256,768]{1,0:T(8,128)S(1)}, f32[256,768]{1,0:T(8,128)}, u32[]{:S(2)}) copy-start(f32[256,768]{1,0:T(8,128)} %get-tuple-element.143) | copy-start | bytes 2359300
  585.2 177.9 %copy-start.1 = (bf16[24,4608]{1,0:T(8,128)(2,1)S(1)}, bf16[24,4608]{1,0:T(8,128)(2,1)}, u32[]{:S(2)}) copy-start(bf16[24,4608]{1,0:T(8,128)(2,1)} %param.21) | copy-start | bytes 663556
  (91 other events, 232.4 us)
Sparse Core Ops, SparseCore 0:
  423.0 162.1 reduce-scatter.4
  591.2 161.5 reduce-scatter.2

commit v4 on v3

--- a/solution.py
+++ b/solution.py
@@ -120,8 +120,9 @@
     return stacked.reshape(mixing.shape).astype(jnp.bfloat16)
 
 
-def forward(inputs, weights, mods, mixer):
+def forward(inputs, weights, table, onehot_own, mixer):
     w_mix, w_out, w_up, w_down = weights
+    mods = jnp.dot(onehot_own, table, precision=lax.Precision.HIGHEST)[:, None, :]
     pieces = jnp.split(mods, 6, axis=2)
     normed = modulate(inputs, pieces[1], pieces[0]).astype(jnp.bfloat16)
     mixing = jnp.dot(normed, w_mix, preferred_element_type=jnp.float32).astype(jnp.bfloat16)
@@ -652,10 +653,469 @@
     return a, d
 
 
-def unpack(a, d):
-    a = a.reshape(8, 768, 768)
+def tile(i, size=256):
+    return pl.ds(pl.multiple_of(size * i, size), size)
+
+
+class Scatter:
+    def __init__(self, grad, came, owns, sems, slots, order, cut):
+        self.grad, self.came, self.owns, self.cut = grad, came, owns, cut
+        self.recv, self.send, self.credit = sems
+        self.slots, self.order = slots, order
+        self.z, self.c, self.y, self.x = place()
+
+    def slot(self, b, p):
+        q = b * len(self.order) + self.order.index(p)
+        return q % self.slots, q >= self.slots, q + self.slots < 2 * len(self.order)
+
+    def window(self, ref, h):
+        rows, _, cols = self.grad.shape[-3:]
+        lead = (slice(None),) * (len(ref.shape) - 3)
+        if self.cut == "cols":
+            return ref.at[(*lead, slice(None), slice(None), pl.ds(h * (cols // 2), cols // 2))]
+        return ref.at[(*lead, pl.ds(h * (rows // 2), rows // 2))]
+
+    def dev(self, z, c, y, x):
+        return (2 * z + c, 2 * y + x)
+
+    def copy(self, src, dst, p, at, to):
+        slot, h, kind = at
+        pltpu.make_async_remote_copy(
+            src_ref=src, dst_ref=dst, send_sem=self.send.at[p, kind], recv_sem=self.recv.at[slot, h, kind],
+            device_id=to, device_id_type=MESH,
+        ).start()
+
+    def arrived(self, ref, slot, h, kind):
+        pltpu.make_async_copy(ref, ref, self.recv.at[slot, h, kind]).wait()
+
+    def may(self, slot, kind, needed):
+        if needed:
+            pl.semaphore_wait(self.credit.at[slot, kind], 1)
+
+    def allow(self, slot, kind, to, needed):
+        if needed:
+            pl.semaphore_signal(self.credit.at[slot, kind], inc=1, device_id=to, device_id_type=MESH)
+
+    def add(self, dst, src, lead):
+        size = 1
+        for d in lead:
+            size *= d
+
+        @pl.loop(0, size)
+        def _(i):
+            at, rest = [], i
+            for d in reversed(lead):
+                at.append(lax.rem(rest, d))
+                rest = rest // d
+            at = tuple(reversed(at))
+            dst.at[at][...] = dst.at[at][...] + src.at[at][...]
+
+    def halves(self, h):
+        z, c, y, x = self.z, self.c, self.y, self.x
+        every = slice(None)
+        to_x, to_y = self.dev(z, c, y, 1 - x), self.dev(z, c, 1 - y, x)
+        if h == 0:
+            return (every, 1 - x), (every, x), (1 - y, x), to_x, to_y
+        return (1 - y, every), (y, every), (y, 1 - x), to_y, to_x
+
+    def r0(self, b, p):
+        slot, wait, _ = self.slot(b, p)
+        self.may(slot, 0, wait)
+        for h in range(2):
+            src = self.window(self.grad.at[p, :, 1 - self.c], h)
+            self.copy(src, self.came[0].at[slot, h], p, (slot, h, 0), self.dev(self.z, 1 - self.c, self.y, self.x))
+
+    def r1(self, b, p):
+        slot, wait, more = self.slot(b, p)
+        for h in range(2):
+            out, _, _, to, _ = self.halves(h)
+            got = self.came[0].at[slot, h]
+            self.arrived(got, slot, h, 0)
+            self.add(self.window(self.grad.at[p, :, self.c], h), got, (4, 2, 2))
+            self.may(slot, 1 + h, wait)
+            src = self.window(self.grad.at[(p, slice(None), self.c, *out)], h)
+            self.copy(src, self.came[1].at[slot, h], p, (slot, h, 1), to)
+        self.allow(slot, 0, self.dev(self.z, 1 - self.c, self.y, self.x), more)
+
+    def r2(self, b, p):
+        slot, wait, more = self.slot(b, p)
+        for h in range(2):
+            _, keep, out, origin, to = self.halves(h)
+            got = self.came[1].at[slot, h]
+            self.arrived(got, slot, h, 1)
+            self.add(self.window(self.grad.at[(p, slice(None), self.c, *keep)], h), got, (4, 2))
+            self.allow(slot, 1 + h, origin, more)
+            self.may(slot, 3 + h, wait)
+            src = self.window(self.grad.at[(p, slice(None), self.c, *out)], h)
+            self.copy(src, self.came[2].at[slot, h], p, (slot, h, 2), to)
+
+    def r3(self, b, p):
+        slot, wait, more = self.slot(b, p)
+        for k in (1, 2, 3):
+            self.may(slot, 4 + k, wait)
+        for h in range(2):
+            _, _, _, _, origin = self.halves(h)
+            got = self.came[2].at[slot, h]
+            self.arrived(got, slot, h, 2)
+            self.add(self.window(self.grad.at[p, :, self.c, self.y, self.x], h), got, (4,))
+            self.allow(slot, 3 + h, origin, more)
+            for k in (1, 2, 3):
+                zz = lax.rem(self.z + k, 4)
+                src = self.window(self.grad.at[p, zz, self.c, self.y, self.x], h)
+                self.copy(
+                    src, self.came[3].at[slot, h, k - 1], p, (slot, h, 2 + k), self.dev(zz, self.c, self.y, self.x)
+                )
+
+    def r4(self, b, p):
+        slot, _, more = self.slot(b, p)
+        for h in range(2):
+            total = self.window(self.grad.at[p, self.z, self.c, self.y, self.x], h)[...].astype(F32)
+            for k in (1, 2, 3):
+                got = self.came[3].at[slot, h, k - 1]
+                self.arrived(got, slot, h, 2 + k)
+                total = total + got[...].astype(F32)
+            self.window(self.owns[b].at[p], h)[...] = total
+        for k in (1, 2, 3):
+            zz = lax.rem(self.z + 4 - k, 4)
+            self.allow(slot, 4 + k, self.dev(zz, self.c, self.y, self.x), more)
+
+    def sent(self, p):
+        g = self.grad
+        refs = [g.at[p, :, 0], g.at[p, :, 0, 0], g.at[p, :, 0, 0, 0]] + [g.at[p, 0, 0, 0, 0]] * 3
+        for kind, ref in enumerate(refs):
+            pltpu.make_async_copy(ref, ref, self.send.at[p, kind]).wait()
+
+
+def active_back_into(normed, weight, down, u, grad_out, active, grad_hidden):
+    @pl.loop(0, 6)
+    def _(t):
+        i = lax.rem(t, 3)
+        rows = tile(t // 3, 128)
+        h = dot(normed[rows, :], weight[4 + u, :, tile(i)])
+        at = tile(3 * u + i)
+        square = h * h
+        t = jnp.tanh(0.7978845608028654 * h * (1.0 + 0.044715 * square))
+        active[rows, at] = (0.5 * h * (1.0 + t)).astype(BF)
+        slope = 0.5 * (1.0 + t) + 0.5 * h * (1.0 - t * t) * (
+            0.7978845608028654 * (1.0 + 3.0 * 0.044715 * square)
+        )
+        grad = dot_nt(grad_out[rows, 0:256], down[0, at, :])
+        grad += dot_nt(grad_out[rows, 256:512], down[1, at, :])
+        grad += dot_nt(grad_out[rows, 512:768], down[2, at, :])
+        grad_hidden[rows, at] = (slope * grad).astype(BF)
+
+
+def norm_back(x, grad_out, mods, scale, k_shift, k_scale, grad, sums):
+    gain = 1.0 + mods[scale]
+
+    def body(i, carry):
+        rows = pl.ds(32 * i, 32)
+        value, factor = unit(x[rows, :].astype(F32))
+        g = grad_out[rows, :]
+        by_scale = carry[0] + jnp.sum(value * g, axis=0, keepdims=True)
+        by_shift = carry[1] + jnp.sum(g, axis=0, keepdims=True)
+        g = g * gain
+        mean = jnp.mean(g, axis=-1, keepdims=True)
+        along = jnp.mean(g * value, axis=-1, keepdims=True)
+        grad[rows, :] = grad[rows, :] + factor * (g - mean - value * along)
+        return by_scale, by_shift
+
+    none = jnp.zeros((1, 768), F32)
+    by_scale, by_shift = lax.fori_loop(0, 8, body, (none, none))
+    row = slice(mods.row, mods.row + 1)
+    sums[row, 768 * k_scale : 768 * k_scale + 768] = by_scale
+    sums[row, 768 * k_shift : 768 * k_shift + 768] = by_shift
+
+
+def gated_into(grad, mods, k, out):
+    gate = mods[k]
+
+    @pl.loop(0, 8)
+    def _(i):
+        rows = pl.ds(32 * i, 32)
+        out[rows, :] = (gate * grad[rows, :]).astype(BF)
+
+
+def gate_grad(left, weight_of, grad, mods, k, sums):
+    for t in range(3):
+        cols = slice(256 * t, 256 * t + 256)
+        total = jnp.zeros((1, 256), F32)
+        for i in range(2):
+            rows = slice(128 * i, 128 * i + 128)
+            total += jnp.sum(dot(left[rows, :], weight_of(t)) * grad[rows, cols], axis=0, keepdims=True)
+        sums[mods.row : mods.row + 1, 768 * k + 256 * t : 768 * k + 256 * t + 256] = total
+
+
+def attend_back(mix, bias, grad_att, grad_mix, first, last):
+    @pl.loop(first, last)
+    def _(j):
+        at = [pl.ds(pl.multiple_of(128 * j + 768 * k, 128), 128) for k in range(3)]
+        keys, values = mix[:, at[1]], mix[:, at[2]]
+        grad_keys, grad_values = jnp.zeros((256, 128), F32), jnp.zeros((256, 128), F32)
+        for i in range(2):
+            rows = slice(128 * i, 128 * i + 128)
+            queries = mix[rows, at[0]] * jnp.asarray(0.125, BF)
+            both = []
+            for e in range(2):
+                que, out = head_lanes(queries, e), head_lanes(grad_att[rows, at[0]], e)
+                probs = softmax(que, keys, bias[rows, :])
+                grad = dot_nt(out, values)
+                grad = (probs * (grad - jnp.sum(grad * probs, axis=-1, keepdims=True))).astype(BF)
+                grad_values += dot_tn(probs.astype(BF), out)
+                grad_keys += dot_tn(grad, que)
+                both.append(dot(grad, keys))
+            lane = lax.broadcasted_iota(jnp.int32, both[0].shape, 1)
+            grad_mix[rows, at[0]] = (0.125 * jnp.where(lane < 64, both[0], both[1])).astype(BF)
+        grad_mix[:, at[1]] = grad_keys.astype(BF)
+        grad_mix[:, at[2]] = grad_values.astype(BF)
+
+
+def outer_into(left, right, base, out, p):
+    @pl.loop(0, 9)
+    def _(t):
+        i, k = t // 3, lax.rem(t, 3)
+        rows, cols = tile(i), tile(k)
+        out[p, rows, cols] = dot_tn(left[:, rows], right[:, tile(base // 256 + k)]).astype(BF)
+
+
+def outer_down_into(active, grad_out, d, out):
+    @pl.loop(0, 12)
+    def _(i):
+        out[d, tile(i), :] = dot_tn(active[:, tile(i)], grad_out[:, 256 * d : 256 * d + 256]).astype(BF)
+
+
+def through_into(left, count, weight, base, out):
+    @pl.loop(0, 6)
+    def _(t):
+        rows, cols = tile(t // 3, 128), tile(lax.rem(t, 3))
+        total = dot_nt(left[rows, 0:768], weight[base, cols, :])
+        for u in range(1, count):
+            total += dot_nt(left[rows, 768 * u : 768 * u + 768], weight[base + u, cols, :])
+        out[rows, cols] = total.astype(out.dtype)
+
+
+A_ORDER, D_ORDER = (4, 5, 6, 7, 3, 0, 1, 2), (0, 1, 2)
+A_SLOTS, D_SLOTS = 4, 3
+
+
+def backward_kernel(
+    tokens, first, cotangent, mods, pick, space_bias, time_bias, mix_s, att_s, mix_t, att_t,
+    A_s, D_s, A_t, D_t,
+    grad_in, table, own_as, own_ds, own_at, own_dt,
+    wa, wd, ga, gd, a0, a1, a2, a3, d0, d1, d2, d3, acc, came, sums,
+    normed, middle, normed_b, active, grad_hidden, grad_out, grad_norm, grad_own, grad_far, mix_own, mix_far,
+    ra, sa, ca, rd, sd, cd, ts, tr, hop, la, ld,
+):
+    def fetch_a(src, pieces):
+        for p in pieces:
+            pltpu.make_async_copy(src.at[p], wa.at[p], la.at[p]).start()
+
+    def fetch_d(src):
+        for p in range(3):
+            pltpu.make_async_copy(src.at[p], wd.at[p], ld.at[p]).start()
+
+    def have_a(*pieces):
+        for p in pieces:
+            pltpu.make_async_copy(A_t.at[p], wa.at[p], la.at[p]).wait()
+
+    def have_d():
+        for p in range(3):
+            pltpu.make_async_copy(D_t.at[p], wd.at[p], ld.at[p]).wait()
+
+    fetch_a(A_t, (3, 4, 5, 6, 7))
+    fetch_d(D_t)
+    fetch_a(A_t, (0, 1, 2))
+    greet()
+    big = Scatter(ga, (a0, a1, a2, a3), (own_at, own_as), (ra, sa, ca), A_SLOTS, A_ORDER, "cols")
+    down = Scatter(gd, (d0, d1, d2, d3), (own_dt, own_ds), (rd, sd, cd), D_SLOTS, D_ORDER, "rows")
+    units = [(s, b, p) for b in range(2) for s in (down, big) for p in s.order]
+    count = [0] * 5
+    total = Total(acc, came, ts, tr)
+
+    def run_stage(stage, unit):
+        s, b, p = unit
+        getattr(s, "r%d" % stage)(b, p)
+
+    def tick():
+        before = list(count)
+        for stage in (1, 2, 3, 4):
+            if count[stage] < before[stage - 1]:
+                run_stage(stage, units[count[stage]])
+                count[stage] += 1
+
+    def ready(s, b, p):
+        if b == 1:
+            s.sent(p)
+
+    def go():
+        run_stage(0, units[count[0]])
+        count[0] += 1
+        tick()
+
+    def flat(ref):
+        return ref.reshape(256, ref.shape[-1])
+
+    weight, lower = wa.reshape(8, 768, 768), wd.reshape(3, 3072, 256)
+    out_a, out_d = ga.reshape(8, 768, 768), gd.reshape(3, 3072, 256)
+    grad = grad_in
+
+    @pl.loop(0, 8)
+    def _(i):
+        rows = pl.ds(32 * i, 32)
+        grad[rows, :] = cotangent[rows, :].astype(F32)
+
+    def up_pieces(b):
+        for u in range(4):
+            ready(big, b, 4 + u)
+            outer_into(normed_b, grad_hidden, 768 * u, out_a, 4 + u)
+            go()
+
+    def out_piece(b, att):
+        ready(big, b, 3)
+        outer_into(att, grad_out, 0, out_a, 3)
+        go()
+
+    def block(b, x, mix, att, bias):
+        vec = Mods(mods, 1 - b)
+        norm_into(x, vec, 0, 1, normed)
+        have_a(3)
+        middle_into(x, att, weight, vec, middle)
+        norm_into(middle, vec, 3, 4, normed_b)
+        gated_into(grad, vec, 5, grad_out)
+        have_a(4, 5, 6, 7)
+        have_d()
+        for u in range(4):
+            active_back_into(normed_b, weight, lower, u, grad_out, active, grad_hidden)
+            if b == 1:
+                tick()
+        for d in range(3):
+            ready(down, b, d)
+            outer_down_into(active, grad_out, d, out_d)
+            go()
+        gate_grad(active, lambda t: lower[t], grad, vec, 5, sums)
+        if b == 0:
+            fetch_d(D_s)
+        else:
+            up_pieces(b)
+        through_into(grad_hidden, 4, weight, 4, grad_norm)
+        if b == 0:
+            fetch_a(A_s, (4, 5, 6, 7))
+        norm_back(middle, grad_norm, vec, 4, 3, 4, grad, sums)
+        gated_into(grad, vec, 2, grad_out)
+        gate_grad(att, lambda t: weight[3, :, 256 * t : 256 * t + 256], grad, vec, 2, sums)
+        through_into(grad_out, 1, weight, 3, flat(grad_own))
+        if b == 0:
+            fetch_a(A_s, (3,))
+            away = Spread(grad_own, grad_far, (hop.at[0], hop.at[1], hop.at[2]))
+            away.start()
+            up_pieces(b)
+            out_piece(b, att)
+            away.wait()
+            attend_back(mix, bias, flat(grad_far), flat(mix_far), 0, 6)
+            home = Spread(mix_far, mix_own, (hop.at[3], hop.at[4], hop.at[5]))
+            home.start()
+            tick()
+            tick()
+            home.wait()
+        else:
+            out_piece(b, att)
+            attend_back(mix, bias, flat(grad_own), flat(mix_own), 0, 3)
+            tick()
+            attend_back(mix, bias, flat(grad_own), flat(mix_own), 3, 6)
+            tick()
+        have_a(0, 1, 2)
+        for j in range(3):
+            ready(big, b, j)
+            outer_into(normed, flat(mix_own), 768 * j, out_a, j)
+            go()
+        through_into(flat(mix_own), 3, weight, 0, grad_norm)
+        if b == 0:
+            fetch_a(A_s, (0, 1, 2))
+        norm_back(x, grad_norm, vec, 1, 0, 1, grad, sums)
+
+    block(0, first, flat(mix_t), flat(att_t), time_bias)
+    block(1, tokens, flat(mix_s), flat(att_s), space_bias)
+    acc[0] = pick[:, 0:1] * sums[0:1, :] + pick[:, 1:2] * sums[1:2, :]
+    total.begin()
+    for i in range(5):
+        tick()
+        total.step(i)
+    while count[4] < len(units):
+        tick()
+    table[...] = acc[5]
+    total.finish()
+    for p in A_ORDER:
+        big.sent(p)
+    for p in D_ORDER:
+        down.sent(p)
+
+
+def backward_all(tokens, cotangent, pick, space_bias, time_bias, saved):
+    shape = jax.ShapeDtypeStruct
+    first, _, mods, mix_s, att_s, mix_t, att_t, *weights = saved
+    anywhere, vmem = pl.BlockSpec(memory_space=pl.ANY), pl.BlockSpec(memory_space=pltpu.VMEM)
+    dma, mem = pltpu.SemaphoreType.DMA, pltpu.VMEM
+    big, down = (8, 4, 2, 2, 2, 3, 8, 768), (3, 4, 2, 2, 2, 12, 8, 256)
+
+    def places(count, block):
+        return [
+            mem((count, 2, 4, 2, 2, *block), BF),
+            mem((count, 2, 4, 2, *block), BF),
+            mem((count, 2, 4, *block), BF),
+            mem((count, 2, 3, *block), BF),
+        ]
+
+    own_a, own_d = shape((8, 3, 8, 768), F32), shape((3, 12, 8, 256), F32)
+    table = (pick.shape[0], 4608)
+    return pl.pallas_call(
+        backward_kernel,
+        out_shape=(shape((256, 768), F32), shape(table, F32), own_a, own_d, own_a, own_d),
+        in_specs=[vmem] * 11 + [anywhere] * 4,
+        out_specs=(vmem,) * 6,
+        scratch_shapes=[
+            mem((8, 4, 2, 4, 3, 8, 768), BF),
+            mem((3, 4, 2, 4, 12, 8, 256), BF),
+            mem(big, BF),
+            mem(down, BF),
+            *places(A_SLOTS, (3, 8, 384)),
+            *places(D_SLOTS, (6, 8, 256)),
+            mem((6, *table), F32),
+            mem((5, *table), F32),
+            mem((8, 4608), F32),
+            mem((256, 768), BF),
+            mem((256, 768), F32),
+            mem((256, 768), BF),
+            mem((256, 3072), BF),
+            mem((256, 3072), BF),
+            mem((256, 768), BF),
+            mem((256, 768), F32),
+            mem((32, 8, 768), BF),
+            mem((32, 8, 768), BF),
+            mem((32, 8, 2304), BF),
+            mem((32, 8, 2304), BF),
+            dma((A_SLOTS, 2, 6)),
+            dma((8, 6)),
+            pltpu.SemaphoreType.REGULAR((A_SLOTS, 8)),
+            dma((D_SLOTS, 2, 6)),
+            dma((3, 6)),
+            pltpu.SemaphoreType.REGULAR((D_SLOTS, 8)),
+            dma((5,)),
+            dma((5,)),
+            dma((6,)),
+            dma((8,)),
+            dma((3,)),
+        ],
+        name="backward_blocks",
+        compiler_params=pltpu.CompilerParams(
+            collective_id=2, has_side_effects=True, vmem_limit_bytes=61 * 2**20
+        ),
+    )(tokens, first, cotangent, mods, pick, space_bias, time_bias, mix_s, att_s, mix_t, att_t, *weights)
+
+
+def owned_grads(a, d):
+    a = a.reshape(8, 24, 768)
+    d = d.reshape(3, 96, 768 // 3)
     wide = [jnp.concatenate([a[p] for p in group], axis=1) for group in ((0, 1, 2), (3,), (4, 5, 6, 7))]
-    d = d.reshape(3, 3072, 256)
     return (*wide, jnp.concatenate([d[0], d[1], d[2]], axis=1))
 
 
@@ -741,7 +1201,6 @@
         and spacemixing.shape == (24, 2304)
         and spacereduce.shape == (96, 768)
     )
-    start = tokens.astype(jnp.float32).reshape(frames_own, patches, width)
     if ours:
         own_clip = onehot_own[0]
         none = jnp.zeros_like(own_clip)
@@ -762,41 +1221,48 @@
         saved = forward_all(
             tokens, partial, pick, space_bias, time_bias, pack(*space_shards), pack(*time_shards)
         )
-        space_full, time_full = unpack(*saved[7:9]), unpack(*saved[9:11])
-        rows = saved[2]
-        space_mods, time_mods = rows[0:1, None, :], rows[1:2, None, :]
+        grad_start, summed, *owned = backward_all(
+            tokens, cotangent, pick, space_bias, time_bias, saved
+        )
+        first, second = saved[:2]
+        summed = summed.astype(jnp.bfloat16)
+        space_own, time_own = owned_grads(*owned[:2]), owned_grads(*owned[2:])
+        space_grads = (
+            *modulation_grads(summed[:clips], cond, spacemodulation, spaceoffsets, here),
+            *space_own,
+        )
+        time_grads = (
+            *modulation_grads(summed[clips:], cond, timemodulation, timeoffsets, here),
+            *time_own,
+        )
     else:
         tables = lax.psum(partial, ("wide", "narrow"))
-        space_full, time_full = fetch(space_shards), fetch(time_shards)
-        own_table = lambda table: jnp.dot(onehot_own, table, precision=lax.Precision.HIGHEST)
-        space_mods = own_table(tables[:clips])[:, None, :]
-        time_mods = own_table(tables[clips:])[:, None, :]
-    first, space_kept = forward(start, space_full, space_mods, space_mixer)
-    if ours:
-        first = saved[0].reshape(start.shape)
-    second, time_kept = forward(first, time_full, time_mods, time_mixer)
-    if ours:
-        second = saved[1].reshape(start.shape)
-    upstream = cotangent.astype(jnp.float32).reshape(frames_own, patches, width)
-    grad_first, time_frames, time_raw = backward(
-        time_kept, time_full, upstream, onehot_own, time_mixer
-    )
-    time_own = scatter(time_raw)
-    grad_start, space_frames, space_raw = backward(
-        space_kept, space_full, grad_first, onehot_own, space_mixer
-    )
-    space_own = scatter(space_raw)
-    summed = lax.psum(
-        jnp.concatenate([space_frames, time_frames], axis=0), ("wide", "narrow")
-    ).astype(jnp.bfloat16)
-    space_grads = (
-        *modulation_grads(summed[:clips], cond, spacemodulation, spaceoffsets, here),
-        *space_own,
-    )
-    time_grads = (
-        *modulation_grads(summed[clips:], cond, timemodulation, timeoffsets, here),
-        *time_own,
-    )
+        space_table, time_table = tables[:clips], tables[clips:]
+        start = tokens.astype(jnp.float32).reshape(frames_own, patches, width)
+        space_full = fetch(space_shards)
+        time_full = fetch(time_shards)
+        first, space_kept = forward(start, space_full, space_table, onehot_own, space_mixer)
+        second, time_kept = forward(first, time_full, time_table, onehot_own, time_mixer)
+        upstream = cotangent.astype(jnp.float32).reshape(frames_own, patches, width)
+        grad_first, time_frames, time_raw = backward(
+            time_kept, time_full, upstream, onehot_own, time_mixer
+        )
+        time_own = scatter(time_raw)
+        grad_start, space_frames, space_raw = backward(
+            space_kept, space_full, grad_first, onehot_own, space_mixer
+        )
+        space_own = scatter(space_raw)
+        summed = lax.psum(
+            jnp.concatenate([space_frames, time_frames], axis=0), ("wide", "narrow")
+        ).astype(jnp.bfloat16)
+        space_grads = (
+            *modulation_grads(summed[:clips], cond, spacemodulation, spaceoffsets, here),
+            *space_own,
+        )
+        time_grads = (
+            *modulation_grads(summed[clips:], cond, timemodulation, timeoffsets, here),
+            *time_own,
+        )
     return (
         first.reshape(-1, width),
         second.reshape(-1, width),

time: 782 us -> 492 us (0.63); the launches traced: 770 us -> 492 us
  Pallas kernels: 190 us -> 460 us
  waiting for transfers between devices: 236 us -> 0 us
  local copies, waits for them, and re-layouts: 119 us -> 12.1 us
  matrix products: 86.3 us -> 5.69 us
  other arithmetic: 64.9 us -> 12.8 us
  blocking collectives: 42.6 us -> 0 us
  starting transfers between devices: 15.7 us -> 0 us
  between operations: 16.5 us -> 0.85 us
    pallas_call x0 -> x1, Pallas kernels: none -> 270 us  [backward_all(): pl.pallas_call(backward_kernel, out_shape=(shape((256, 768), F32), shape(...]
    reduce_scatter x2 -> x0, waiting for transfers between devices: 180 us -> none  [scatter(): lax.psum_scatter(packed, ('wide', 'narrow'), scatter_dimension=0, tiled=T...]
    dot_general x36 -> x0, matrix products: 80.8 us -> none  [the longest x8 28.7 us: outer(): jnp.einsum('fpa,fpb->ab', left, right, preferred_element_type=jnp.float32)]
    all_to_all x4 -> x0, waiting for transfers between devices: 55.5 us -> none  [the longest x1 28.7 us: time_in(): lax.all_to_all(mixing, ('wide', 'narrow'), split_axis=1, concat_axis=0, t...]
    psum x1 -> x0, blocking collectives: 42.6 us -> none  [per_device(): lax.psum(jnp.concatenate([space_frames, time_frames], axis=0), ('wide', '...]
    unnamed x285 -> x21, local copies, waits for them, and re-layouts: 30.4 us -> 2.78 us
    reshape x5 -> x0, local copies, waits for them, and re-layouts: 25.5 us -> none  [the longest x2 17 us: scatter(): g.astype(jnp.bfloat16).reshape(rows, -1)]
    slice x5 -> x0, local copies, waits for them, and re-layouts: 21.6 us -> none  [the longest x2 13.8 us: unpack(): a[p]]
  transfers between devices with their start and end apart: 6 -> 0, of which waited for: 6 -> 0; matrix products, arithmetic and copies ran while one was open for 16% -> 0% of each run, Pallas kernels for 0% -> 0%
where the time goes in v4:
time: 492 us
  Pallas kernels  460 us (93%)
  other arithmetic  12.8 us (3%)
  local copies, waits for them, and re-layouts  12.1 us (2%)
  matrix products  5.69 us (1%)
    pallas_call x1, Pallas kernels, backward_all(): pl.pallas_call(backward_kernel, out_shape=(shape((256, 768), F32), shape(...  270 us
    pallas_call x1, Pallas kernels, forward_all(): pl.pallas_call(forward_kernel, out_shape=(plane, plane, shape((8, 4608),...  190 us

profile of v4, /device:TPU:0, one launch (start us, length us, event | category | flops | bytes accessed | tf_op | source)
XLA Modules:
  0.0 491.7 jit_solution(2282944917799123117)
XLA Ops:
  0.6 0.0 copy-start
  0.7 0.0 copy-start.6
  0.7 0.9 convert_dynamic-update-slice_fusion.1
  1.6 0.9 convolution_add_fusion.1
  2.5 0.8 convert_dynamic-update-slice_fusion
  3.3 1.2 convolution_add_fusion
  4.5 0.7 pad_maximum_fusion.8.table
  5.2 0.8 dynamic-slice_compare_fusion
  6.0 0.1 or.23
  6.1 0.7 compare_reduce_fusion
  6.8 0.8 reduce-window.8
  7.6 0.1 convert_reduce_fusion.2
  7.7 0.1 broadcast_in_dim.17
  7.8 0.1 eq.76
  7.9 0.1 eq.72
  8.0 0.9 fusion.2
  8.9 0.6 dynamic-slice
  9.5 0.6 fusion.10
  10.1 0.1 pad_bitcast_fusion.1
  10.2 0.7 copy.50.pick
  10.9 1.0 pad_maximum_fusion.1
  11.9 0.1 copy.60
  12.0 1.0 pad_maximum_fusion
  13.0 0.1 copy.61
  13.0 0.9 copy_bitcast_fusion.2
  14.0 0.1 reshape.149
  14.0 0.1 reshape.151
  14.1 0.7 copy_bitcast_fusion.4
  14.9 189.7 %forward_blocks.1 = (f32[256,768]{1,0:T(8,128)}, f32[256,768]{1,0:T(8,128)}, f32[8,4608]{1,0:T(8,128)}, bf16[32,8,2304]{2,1,0:T(8,128)(2,1)}, bf16[32,8,768]{2,1...) custom-call(bf16[256,768]{1,0:T(8,128)(2,1)} %tokens.3, ...), custom_call_target="tpu_custom_call" | custom-call | tf_op jit(solution)/shard_map/forward_blocks/pallas_call | solution.py:619
  204.6 270.4 %backward_blocks.1 = (f32[256,768]{1,0:T(8,128)}, f32[8,4608]{1,0:T(8,128)}, f32[8,3,8,768]{3,2,1,0:T(8,128)}, f32[3,12,8,256]{3,2,1,0:T(8,128)}, f32[8,3,8,768]{3,2,1,0:T(8,128)}, /*index=5*/f32[3,12,8,256]{3,2,1,0:T(8,128)}) custom-call(bf16[256,768]{1,0:T(8,128)(2,1)} %tokens.3, f32[256,768]{1,0:T(8,128)} %get-tuple-element.96.first, ...), custom_call_target="tpu_custom_call" | custom-call | tf_op jit(solution)/shard_map/backward_blocks/pallas_call | solution.py:1070
  475.1 1.1 slice_bitcast_fusion.2
  476.2 0.7 pad_maximum_fusion.5
  476.9 1.8 slice_bitcast_fusion.9
  478.8 0.7 pad_maximum_fusion.4
  479.5 0.7 pad_maximum_fusion.7
  480.2 1.0 slice_bitcast_fusion.5
  481.2 0.7 pad_maximum_fusion.3
  481.9 0.7 slice_bitcast_fusion.17
  482.6 0.7 pad_maximum_fusion.2
  483.3 0.7 pad_maximum_fusion.6
  484.1 1.8 fusion.5
  485.9 1.8 fusion.7
  487.6 0.1 convert_reduce_fusion
  487.7 0.6 dynamic_slice.25
  488.4 0.6 dynamic_slice.26
  489.0 0.9 copy.67
  489.9 0.9 copy.68
  490.8 0.9 copy.69
  (19 shorter events, 0.1 us)
Async XLA Ops:
  0.6 1.0 copy-start
  0.7 13.3 %copy-start.6 = (bf16[96,768]{1,0:T(8,128)(2,1)S(1)}, bf16[96,768]{1,0:T(8,128)(2,1)}, u32[]{:S(2)}) copy-start(bf16[96,768]{1,0:T(8,128)(2,1)} %param.26) | copy-start | bytes 442372
  0.7 13.4 %copy-start.7 = (bf16[96,768]{1,0:T(8,128)(2,1)S(1)}, bf16[96,768]{1,0:T(8,128)(2,1)}, u32[]{:S(2)}) copy-start(bf16[96,768]{1,0:T(8,128)(2,1)} %param.32) | copy-start | bytes 442372
  475.0 6.9 %copy-start.4 = (f32[8,3,8,768]{3,2,1,0:T(8,128)S(1)}, f32[8,3,8,768]{3,2,1,0:T(8,128)}, u32[]{:S(2)}) copy-start(f32[8,3,8,768]{3,2,1,0:T(8,128)} %get-tuple-element.45) | copy-start | bytes 1769476
  475.1 9.0 %copy-start.5 = (f32[8,4608]{1,0:T(8,128)S(1)}, f32[8,4608]{1,0:T(8,128)}, u32[]{:S(2)}) copy-start(f32[8,4608]{1,0:T(8,128)} %get-tuple-element.44) | copy-start | bytes 442372
  475.1 14.0 %copy-start.1 = (f32[256,768]{1,0:T(8,128)S(1)}, f32[256,768]{1,0:T(8,128)}, u32[]{:S(2)}) copy-start(f32[256,768]{1,0:T(8,128)} %get-tuple-element.96.first) | copy-start | bytes 2359300
  476.2 13.7 %copy-start.2 = (f32[256,768]{1,0:T(8,128)S(1)}, f32[256,768]{1,0:T(8,128)}, u32[]{:S(2)}) copy-start(f32[256,768]{1,0:T(8,128)} %get-tuple-element.97) | copy-start | bytes 2359300
  478.7 12.0 %copy-start.3 = (f32[256,768]{1,0:T(8,128)S(1)}, f32[256,768]{1,0:T(8,128)}, u32[]{:S(2)}) copy-start(f32[256,768]{1,0:T(8,128)} %get-tuple-element.98) | copy-start | bytes 2359300
